TPU v7x, 1024 devices: a whole 8x8x8 slice. The times are simulated.
1024 devices in a mesh: dp: 16 (over z, x_lo), mp: 64 (over y, x_hi, core).
Axes of the slice: x: 8 (x_hi: 4, x_lo: 2; x = x_hi * 2 + x_lo), y: 8, z: 8, core: 2. Of those that a mesh axis runs over, the one named last changes fastest.
Arguments:
- grad_parts: bfloat16 [16, 32, 1024, 1024], P('dp', None, 'mp'), may hold values from -5 to 5
- momentum: float32 [32, 1024, 1024], P('dp', 'mp'), may hold values from -3 to 3
- second_moment: float32 [32, 1024, 1024], P('dp', 'mp'), may hold values from 0.02 to 0.5
- left_basis: bfloat16 [32, 1024, 1024], P('dp'), may hold values from -1 to 2
- right_basis: bfloat16 [32, 1024, 1024], P('dp'), may hold values from -1 to 2
- lr_scale: float32 [32], P('dp'), may hold values from 0.25 to 1
Outputs:
- update: float32 [32, 1024, 1024], P('dp', 'mp')
- momentum_out: float32 [32, 1024, 1024], P('dp', 'mp')
- second_out: float32 [32, 1024, 1024], P('dp', 'mp')
All inputs are finite; a program needn't handle non-finite values.
Results may differ from a plain program's by a relative error of at most 0.023.
Values may be sent and summed in bfloat16 or wider, within the bound.
No kernel may reach another device: no remote copies, remote signals or barrier semaphores. Data moves between devices by JAX's collectives and lax.ppermute only.
A program may use at most 32 MiB of HBM per device.

v0:
```python
import jax
import jax.numpy as jnp
from jax import lax
from jax.sharding import PartitionSpec as P

beta_one = 0.95
beta_two = 0.95
epsilon = 1e-08
bias_one = 1.0 - 0.95**10
bias_two = 1.0 - 0.95**10


def turn_left(grad_sum, moment, left):
    moment_new = beta_one * moment + (1.0 - beta_one) * grad_sum
    stacked = jnp.stack([grad_sum.astype(jnp.bfloat16), moment_new.astype(jnp.bfloat16)], axis=1)
    turned = jnp.einsum("bik,bxji->bxkj", left, stacked, preferred_element_type=jnp.float32)
    return (turned.astype(jnp.bfloat16), moment_new)


def local(grad_parts, momentum, second_moment, left_basis, right_basis, lr_scale):
    grad_sum = lax.psum_scatter(grad_parts[0], "dp", scatter_dimension=0, tiled=True).astype(
        jnp.float32
    )
    turned, momentum_out = turn_left(grad_sum, momentum, left_basis)
    arrived = lax.all_to_all(turned, "mp", split_axis=2, concat_axis=3, tiled=True)
    rotated = jnp.einsum("bxkj,bjl->bxkl", arrived, right_basis, preferred_element_type=jnp.float32)
    rotated_grad = rotated[:, 0]
    rotated_moment = rotated[:, 1]
    second_out = beta_two * second_moment + (1.0 - beta_two) * rotated_grad * rotated_grad
    ratio = (rotated_moment / bias_one / (jnp.sqrt(second_out / bias_two) + epsilon)).astype(
        jnp.bfloat16
    )
    returned = jnp.einsum(
        "bkl,bjl->bkj", ratio, right_basis, preferred_element_type=jnp.float32
    ).astype(jnp.bfloat16)
    landed = lax.all_to_all(returned, "mp", split_axis=2, concat_axis=1, tiled=True)
    full_step = jnp.einsum("bik,bkj->bji", left_basis, landed, preferred_element_type=jnp.float32)
    update = lr_scale[:, None, None] * full_step
    return (update, momentum_out, second_out)


def solution(mesh):
    in_specs = (
        P("dp", None, "mp", None),
        P("dp", "mp", None),
        P("dp", "mp", None),
        P("dp", None, None),
        P("dp", None, None),
        P("dp"),
    )
    out_specs = (P("dp", "mp", None), P("dp", "mp", None), P("dp", "mp", None))
    return jax.shard_map(local, mesh=mesh, in_specs=in_specs, out_specs=out_specs, check_vma=False)
```

profile of v0, /device:TPU:1, one launch (start us, length us, event | category | flops | bytes accessed | tf_op | source)
XLA Modules:
  0.0 171.7 jit_solution(12727884295344393791)
XLA Ops:
  7.2 0.0 reduce-scatter.2.cloned.1.call-start
  7.2 0.7 reduce-scatter.2.cloned.1.call-update
  7.9 84.4 %reduce-scatter.2.cloned.1.call-done = bf16[2,16,1024]{2,1,0:T(8,128)(2,1)} async-done(((bf16[32,16,1024]{2,1,0:T(8,128)(2,1)}), bf16[2,16,1024]{2,1,0:T(8,128)(2,1)}) %reduce-scatter.2.cloned.1.call-update) | async-done | bytes 65552 | tf_op jit(solution)/shard_map/reduce_scatter | solution.py:21
  92.3 1.6 convert_bitcast_fusion
  93.9 3.0 %fusion.7 = bf16[2,2,1024,16]{2,3,1,0:T(8,128)(2,1)S(1)} fusion(bf16[2,1024,1024]{2,1,0:T(8,128)(2,1)} %param.9, bf16[2,1,16,1024]{3,2,1,0:T(8,128)(2,1)S(1)} %get-tuple-element.3, bf16[2,1,16,1024]{3,2,1,0:T(8,128)(2,1)} %bitcast.61), kind=kOutput, calls=%fused_computation.5 | convolution fusion | flops 134348800 | bytes 4456448 | tf_op jit(solution)/shard_map/bik,bxji->bxkj/dot_general | solution.py:16
  97.0 0.7 copy.20
  97.7 1.1 reshape.11
  98.8 36.0 %all_to_all.36 = bf16[64,2,512]{2,1,0:T(2,128)(2,1)S(1)} all-to-all(bf16[64,2,512]{2,1,0:T(2,128)(2,1)S(1)} %reshape.11), channel_id=1, replica_groups=mesh['dp'=16,'mp'=64] {'mp'}, dimensions={0} | all-to-all | bytes 262144 | tf_op jit(solution)/shard_map/all_to_all | solution.py:25
  134.9 0.7 reshape.12
  135.6 0.0 copy-start.2
  135.6 0.7 copy.39
  136.3 1.8 %all_to_all.29 = bf16[2,2,16,1024]{3,2,1,0:T(8,128)(2,1)S(1)} reshape(bf16[2,2,16,64,16]{4,3,2,1,0:T(8,128)(2,1)S(1)} %bitcast.56) | data formatting | bytes 262144 | tf_op jit(solution)/shard_map/all_to_all | solution.py:25
  138.0 0.0 copy-start
  138.1 3.2 %fusion.2 = f32[2,2,16,1024]{3,2,0,1:T(8,128)S(1)} fusion(bf16[2,1024,1024]{2,1,0:T(8,128)(2,1)} %param.10, bf16[2,2,16,1024]{3,2,1,0:T(8,128)(2,1)S(1)} %all_to_all.29), kind=kOutput, calls=%fused_computation.2 | convolution fusion | flops 134217728 | bytes 4587520 | tf_op jit(solution)/shard_map/bxkj,bjl->bxkl/dot_general | solution.py:26
  141.2 0.0 copy-done.2
  141.2 0.0 copy-start.3
  141.3 0.2 copy-done
  141.5 0.0 copy-start.1
  141.5 1.2 convolution_convert_fusion
  142.7 0.4 copy.25
  143.1 0.5 reshape.13
  143.5 15.9 %all_to_all.37 = bf16[64,2,256]{2,1,0:T(2,128)(2,1)S(1)} all-to-all(bf16[64,2,256]{2,1,0:T(2,128)(2,1)S(1)} %reshape.13), channel_id=1, replica_groups=mesh['dp'=16,'mp'=64] {'mp'}, dimensions={0} | all-to-all | bytes 131072 | tf_op jit(solution)/shard_map/all_to_all | solution.py:36
  159.5 0.4 reshape.14
  159.9 0.2 copy.40
  160.1 0.8 all_to_all.33
  160.8 0.0 copy-done.3
  160.8 4.0 %convolution_multiply_fusion = f32[2,16,1024]{2,1,0:T(8,128)} fusion(bf16[2,1024,16]{1,2,0:T(8,128)(2,1)S(1)} %all_to_all.33, bf16[2,1024,1024]{2,1,0:T(8,128)(2,1)} %param.9, f32[2]{0:T(128)S(1)} %copy-done.3), kind=kOutput, calls=%fused_computation.6 | convolution fusion | flops 67141632 | bytes 4390920 | tf_op jit(solution)/shard_map/bik,bkj->bji/dot_general | solution.py:37
  164.9 0.0 copy-done.1
  (1 shorter events, 0.0 us)
Async XLA Ops:
  7.2 85.1 %reduce-scatter.2.cloned.1.call-start = ((), (), s32[]{:S(2)}) async-start(), calls=%async_computation.3 | async-start | bytes 1114112 | tf_op jit(solution)/shard_map/reduce_scatter | solution.py:21
  135.6 5.6 %copy-start.2 = (f32[2,16,1024]{2,1,0:T(8,128)S(1)}, f32[2,16,1024]{2,1,0:T(8,128)}, u32[]{:S(2)}) copy-start(f32[2,16,1024]{2,1,0:T(8,128)} %param.8) | copy-start | bytes 393220
  138.0 3.5 %copy-start = (bf16[2,1024,1024]{2,1,0:T(8,128)(2,1)S(1)}, bf16[2,1024,1024]{2,1,0:T(8,128)(2,1)}, u32[]{:S(2)}) copy-start(bf16[2,1024,1024]{2,1,0:T(8,128)(2,1)} %param.10) | copy-start | bytes 12582916
  141.2 19.6 %copy-start.3 = (f32[2]{0:T(128)S(1)}, f32[2]{0:T(128)}, u32[]{:S(2)}) copy-start(f32[2]{0:T(128)} %param.11) | copy-start | bytes 28
  141.5 23.4 %copy-start.1 = (f32[2,16,1024]{2,1,0:T(8,128)}, f32[2,16,1024]{2,1,0:T(8,128)S(1)}, u32[]{:S(2)}) copy-start(f32[2,16,1024]{2,1,0:T(8,128)S(1)} %fusion.10) | copy-start | bytes 393220
Sparse Core Ops, SparseCore 0:
  11.4 80.8 reduce-scatter.1
where the time goes:
time: 172 us
  waiting for transfers between devices  85.1 us (49%)
  blocking collectives  52 us (30%)
  between operations  14.1 us (8%)
  matrix products  11.4 us (7%)
  local copies, waits for them, and re-layouts  7.45 us (4%)
    reduce_scatter x1, waiting for transfers between devices, local(): lax.psum_scatter(grad_parts[0], 'dp', scatter_dimension=0, tiled=True)  84.4 us
    all_to_all x1, blocking collectives, local(): lax.all_to_all(turned, 'mp', split_axis=2, concat_axis=3, tiled=True)  36 us
    all_to_all x1, blocking collectives, local(): lax.all_to_all(returned, 'mp', split_axis=2, concat_axis=1, tiled=True)  15.9 us
    dot_general x1, matrix products, local(): jnp.einsum('bik,bkj->bji', left_basis, landed, preferred_element_type=jnp...  4.05 us
  transfers between devices with their start and end apart: 1, of which 1 were waited for; matrix products, arithmetic and copies ran while one was open for 0% of the time, Pallas kernels for 0%

commit v1 on v0

v1 whole, which is shorter than its diff:
```python
import jax
import jax.numpy as jnp
from jax import lax
from jax.sharding import Mesh, PartitionSpec as P

beta_one = 0.95
beta_two = 0.95
epsilon = 1e-08
bias_one = 1.0 - 0.95**10
bias_two = 1.0 - 0.95**10


MP = ("y", "xh", "c")
DP = ("z", "xl")


def turn_left(grad_sum, moment, left):
    moment_new = beta_one * moment + (1.0 - beta_one) * grad_sum
    stacked = jnp.stack([grad_sum.astype(jnp.bfloat16), moment_new.astype(jnp.bfloat16)], axis=1)
    turned = jnp.einsum("bik,bxji->bxkj", left, stacked, preferred_element_type=jnp.float32)
    return (turned.astype(jnp.bfloat16), moment_new)


def local(grad_parts, momentum, second_moment, left_basis, right_basis, lr_scale):
    parts = grad_parts[0].reshape(8, 2, 2, 16, 1024)
    side = lax.axis_index("xl")
    away = lax.dynamic_index_in_dim(parts, 1 - side, 1, keepdims=False)
    kept = lax.dynamic_index_in_dim(parts, side, 1, keepdims=False)
    came = lax.ppermute(away, "xl", [(0, 1), (1, 0)])
    pair = (kept.astype(jnp.float32) + came.astype(jnp.float32)).astype(jnp.bfloat16)
    shares = lax.all_to_all(pair, "z", split_axis=0, concat_axis=0, tiled=True)
    grad_sum = jnp.sum(shares.astype(jnp.float32), axis=0)
    turned, momentum_out = turn_left(grad_sum, momentum, left_basis)
    arrived = lax.all_to_all(turned, MP, split_axis=2, concat_axis=3, tiled=True)
    rotated = jnp.einsum("bxkj,bjl->bxkl", arrived, right_basis, preferred_element_type=jnp.float32)
    rotated_grad = rotated[:, 0]
    rotated_moment = rotated[:, 1]
    second_out = beta_two * second_moment + (1.0 - beta_two) * rotated_grad * rotated_grad
    ratio = (rotated_moment / bias_one / (jnp.sqrt(second_out / bias_two) + epsilon)).astype(
        jnp.bfloat16
    )
    returned = jnp.einsum(
        "bkl,bjl->bkj", ratio, right_basis, preferred_element_type=jnp.float32
    ).astype(jnp.bfloat16)
    landed = lax.all_to_all(returned, MP, split_axis=2, concat_axis=1, tiled=True)
    full_step = jnp.einsum("bik,bkj->bji", left_basis, landed, preferred_element_type=jnp.float32)
    update = lr_scale[:, None, None] * full_step
    return (update, momentum_out, second_out)


def solution(mesh):
    fine = Mesh(mesh.devices.reshape(8, 2, 8, 4, 2), DP + MP)
    in_specs = (
        P(DP, None, MP, None),
        P(DP, MP, None),
        P(DP, MP, None),
        P(DP, None, None),
        P(DP, None, None),
        P(DP),
    )
    out_specs = (P(DP, MP, None), P(DP, MP, None), P(DP, MP, None))
    return jax.shard_map(local, mesh=fine, in_specs=in_specs, out_specs=out_specs, check_vma=False)
```

time: 172 us -> 115 us (0.67)
  waiting for transfers between devices: 85.1 us -> 7.38 us
  blocking collectives: 52 us -> 80.9 us
  between operations: 14.1 us -> 0.77 us
  starting transfers between devices: 0.04 us -> 3.95 us
    reduce_scatter x1 -> x0, waiting for transfers between devices: 84.4 us -> none  [local(): lax.psum_scatter(grad_parts[0], 'dp', scatter_dimension=0, tiled=True)]
    all_to_all x2 -> x3, blocking collectives: 52 us -> 80.9 us  [the longest x1 35.1 us: local(): shares = lax.all_to_all(pair, 'z', split_axis=0, concat_axis=0, tiled=True)]
    ppermute x0 -> x1, waiting for transfers between devices: none -> 7.38 us  [local(): came = lax.ppermute(away, 'xl', [(0, 1), (1, 0)])]
    ppermute x0 -> x1, starting transfers between devices: none -> 3.95 us  [local(): came = lax.ppermute(away, 'xl', [(0, 1), (1, 0)])]
where the time goes in v1:
time: 115 us
  blocking collectives  80.9 us (70%)
  matrix products  11.4 us (10%)
  local copies, waits for them, and re-layouts  8.58 us (7%)
  waiting for transfers between devices  7.38 us (6%)
  starting transfers between devices  3.95 us (3%)
  other arithmetic  2.02 us (2%)
    all_to_all x1, blocking collectives, local(): shares = lax.all_to_all(pair, 'z', split_axis=0, concat_axis=0, tiled=True)  35.1 us
    all_to_all x1, blocking collectives, local(): lax.all_to_all(turned, MP, split_axis=2, concat_axis=3, tiled=True)  29.7 us
    all_to_all x1, blocking collectives, local(): lax.all_to_all(returned, MP, split_axis=2, concat_axis=1, tiled=True)  16.1 us
    ppermute x1, waiting for transfers between devices, local(): came = lax.ppermute(away, 'xl', [(0, 1), (1, 0)])  7.38 us
    dot_general x1, matrix products, local(): jnp.einsum('bik,bkj->bji', left_basis, landed, preferred_element_type=jnp...  4.05 us
    ppermute x1, starting transfers between devices, local(): came = lax.ppermute(away, 'xl', [(0, 1), (1, 0)])  3.95 us
    dot_general x1, matrix products, local(): jnp.einsum('bxkj,bjl->bxkl', arrived, right_basis, preferred_element_type...  3.16 us
    dot_general x1, matrix products, turn_left(): jnp.einsum('bik,bxji->bxkj', left, stacked, preferred_element_type=jnp.fl...  3.01 us
  transfers between devices with their start and end apart: 1, of which 1 were waited for; matrix products, arithmetic and copies ran while one was open for 0% of the time, Pallas kernels for 0%

profile of v1, /device:TPU:1, one launch (start us, length us, event | category | flops | bytes accessed | tf_op | source)
XLA Modules:
  0.0 115.0 jit_solution(12193618994138692014)
XLA Ops:
  0.6 0.0 copy-start.3
  0.6 1.1 dynamic-slice_bitcast_fusion
  1.8 3.9 %collective-permute-start = (bf16[8,2,16,1024]{3,2,1,0:T(8,128)(2,1)S(1)}, bf16[8,2,16,1024]{3,2,1,0:T(8,128)(2,1)S(1)}, u32[]{:S(2)}, u32[]{:S(2)}) collective-permute-start(bf16[8,2,16,1024]{3,2,1,0:T(8,128)(2,1)S(1)} %dynamic-slice_bitcast_fusion), channel_id=1, source_target_pairs={{0,64},{64,0},{1,65},{65,1},{2,66},{66,2},{3,67},{67,3},{4,68},{68... | collective-permute-start | bytes 1572872 | tf_op jit(solution)/shard_map/ppermute | solution.py:29
  5.7 7.4 %collective-permute-done = bf16[8,2,16,1024]{3,2,1,0:T(8,128)(2,1)S(1)} collective-permute-done((bf16[8,2,16,1024]{3,2,1,0:T(8,128)(2,1)S(1)}, bf16[8,2,16,1024]{3,2,1,0:T(8,128)(2,1)S(1)}, u32[]{:S(2)}, u32[]{:S(2)}) %collective-permute-start) | collective-permute-done | bytes 524320 | tf_op jit(solution)/shard_map/ppermute | solution.py:29
  13.1 1.2 %fusion.10 = bf16[8,2,16,1024]{3,2,1,0:T(8,128)(2,1)S(1)} fusion(bf16[8,2,16,1024]{3,2,1,0:T(8,128)(2,1)S(1)} %collective-permute-done, bf16[8,2,2,16,1024]{4,3,2,1,0:T(8,128)(2,1)} %bitcast.67, s32[]{:T(128)S(6)} %select_n.7), kind=kLoop, calls=%fused_computation.9 | loop fusion | flops 1048576 | bytes 1572868 | tf_op jit(solution)/shard_map/convert_element_type | solution.py:30
  14.3 35.1 %all_to_all.41 = bf16[8,2,16,1024]{3,2,1,0:T(8,128)(2,1)S(1)} all-to-all(bf16[8,2,16,1024]{3,2,1,0:T(8,128)(2,1)S(1)} %fusion.10), channel_id=1, replica_groups=mesh['z'=8,'xl'=2,'y'=8,'xh'=4,'c'=2] {'z'}, dimensions={0} | all-to-all | bytes 1048576 | tf_op jit(solution)/shard_map/all_to_all | solution.py:31
  49.5 0.1 convert_reduce_fusion
  49.6 0.0 copy-done.3
  49.6 0.7 convert_bitcast_fusion
  50.3 3.0 %fusion.7 = bf16[2,2,1024,16]{2,3,1,0:T(8,128)(2,1)S(1)} fusion(bf16[2,1024,1024]{2,1,0:T(8,128)(2,1)} %param.9, bf16[2,1,16,1024]{3,2,1,0:T(8,128)(2,1)S(1)} %get-tuple-element.3, bf16[2,1,16,1024]{3,2,1,0:T(8,128)(2,1)S(1)} %get-tuple-element.5), kind=kOutput, calls=%fused_computation.5 | convolution fusion | flops 134348800 | bytes 4456448 | tf_op jit(solution)/shard_map/bik,bxji->bxkj/dot_general | solution.py:20
  53.3 0.7 copy.20
  54.0 1.1 reshape.22
  55.2 29.7 %all_to_all.42 = bf16[64,2,512]{2,1,0:T(2,128)(2,1)S(1)} all-to-all(bf16[64,2,512]{2,1,0:T(2,128)(2,1)S(1)} %reshape.22), channel_id=1, replica_groups=mesh['z'=8,'xl'=2,'y'=8,'xh'=4,'c'=2] {'y','xh','c'}, dimensions={0} | all-to-all | bytes 262144 | tf_op jit(solution)/shard_map/all_to_all | solution.py:34
  84.8 0.7 reshape.23
  85.5 0.0 copy-start.2
  85.5 0.7 copy.39
  86.2 1.8 %all_to_all.33 = bf16[2,2,16,1024]{3,2,1,0:T(8,128)(2,1)S(1)} reshape(bf16[2,2,16,64,16]{4,3,2,1,0:T(8,128)(2,1)S(1)} %bitcast.62) | data formatting | bytes 262144 | tf_op jit(solution)/shard_map/all_to_all | solution.py:34
  88.0 0.0 copy-start
  88.0 3.2 %fusion.2 = f32[2,2,16,1024]{3,2,0,1:T(8,128)S(1)} fusion(bf16[2,1024,1024]{2,1,0:T(8,128)(2,1)} %param.10, bf16[2,2,16,1024]{3,2,1,0:T(8,128)(2,1)S(1)} %all_to_all.33), kind=kOutput, calls=%fused_computation.2 | convolution fusion | flops 134217728 | bytes 4587520 | tf_op jit(solution)/shard_map/bxkj,bjl->bxkl/dot_general | solution.py:35
  91.2 0.0 copy-done.2
  91.2 0.0 copy-start.4
  91.2 0.2 copy-done
  91.5 0.0 copy-start.1
  91.5 1.2 %convolution_convert_fusion = bf16[2,16,1024]{2,1,0:T(8,128)(2,1)S(1)} fusion(bf16[2,1024,1024]{2,1,0:T(8,128)(2,1)S(1)} %copy-done, f32[2,2,16,1024]{3,2,0,1:T(8,128)S(1)} %fusion.2, f32[2,16,1024]{2,1,0:T(8,128)S(1)} %fusion.11), kind=kOutput, calls=%fused_computation.7 | convolution fusion | flops 67305472 | bytes 4521984 | tf_op jit(solution)/shard_map/bkl,bjl->bkj/dot_general | solution.py:42
  92.7 0.4 copy.25
  93.0 0.5 reshape.24
  93.5 16.1 %all_to_all.43 = bf16[64,2,256]{2,1,0:T(2,128)(2,1)S(1)} all-to-all(bf16[64,2,256]{2,1,0:T(2,128)(2,1)S(1)} %reshape.24), channel_id=1, replica_groups=mesh['z'=8,'xl'=2,'y'=8,'xh'=4,'c'=2] {'y','xh','c'}, dimensions={0} | all-to-all | bytes 131072 | tf_op jit(solution)/shard_map/all_to_all | solution.py:45
  109.6 0.4 reshape.25
  110.0 0.2 copy.40
  110.2 0.8 all_to_all.37
  111.0 0.0 copy-done.4
  111.0 4.0 %convolution_multiply_fusion = f32[2,16,1024]{2,1,0:T(8,128)} fusion(bf16[2,1024,16]{1,2,0:T(8,128)(2,1)S(1)} %all_to_all.37, bf16[2,1024,1024]{2,1,0:T(8,128)(2,1)} %param.9, f32[2]{0:T(128)S(1)} %copy-done.4), kind=kOutput, calls=%fused_computation.6 | convolution fusion | flops 67141632 | bytes 4390920 | tf_op jit(solution)/shard_map/bik,bkj->bji/dot_general | solution.py:46
  115.0 0.0 copy-done.1
  (1 shorter events, 0.0 us)
Async XLA Ops:
  0.6 48.9 %copy-start.3 = (f32[2,16,1024]{2,1,0:T(8,128)S(1)}, f32[2,16,1024]{2,1,0:T(8,128)}, u32[]{:S(2)}) copy-start(f32[2,16,1024]{2,1,0:T(8,128)} %param.7) | copy-start | bytes 393220
  1.8 11.3 %collective-permute-start = (bf16[8,2,16,1024]{3,2,1,0:T(8,128)(2,1)S(1)}, bf16[8,2,16,1024]{3,2,1,0:T(8,128)(2,1)S(1)}, u32[]{:S(2)}, u32[]{:S(2)}) collective-permute-start(bf16[8,2,16,1024]{3,2,1,0:T(8,128)(2,1)S(1)} %dynamic-slice_bitcast_fusion), channel_id=1, source_target_pairs={{0,64},{64,0},{1,65},{65,1},{2,66},{66,2},{3,67},{67,3},{4,68},{68... | collective-permute-start | bytes 1572872 | tf_op jit(solution)/shard_map/ppermute | solution.py:29
  85.5 5.6 %copy-start.2 = (f32[2,16,1024]{2,1,0:T(8,128)S(1)}, f32[2,16,1024]{2,1,0:T(8,128)}, u32[]{:S(2)}) copy-start(f32[2,16,1024]{2,1,0:T(8,128)} %param.8) | copy-start | bytes 393220
  88.0 3.5 %copy-start = (bf16[2,1024,1024]{2,1,0:T(8,128)(2,1)S(1)}, bf16[2,1024,1024]{2,1,0:T(8,128)(2,1)}, u32[]{:S(2)}) copy-start(bf16[2,1024,1024]{2,1,0:T(8,128)(2,1)} %param.10) | copy-start | bytes 12582916
  91.2 19.8 %copy-start.4 = (f32[2]{0:T(128)S(1)}, f32[2]{0:T(128)}, u32[]{:S(2)}) copy-start(f32[2]{0:T(128)} %param.11) | copy-start | bytes 28
  91.5 23.6 %copy-start.1 = (f32[2,16,1024]{2,1,0:T(8,128)}, f32[2,16,1024]{2,1,0:T(8,128)S(1)}, u32[]{:S(2)}) copy-start(f32[2,16,1024]{2,1,0:T(8,128)S(1)} %fusion.11) | copy-start | bytes 393220

commit v2 on v1

v2 whole, which is shorter than its diff:
```python
import jax
import jax.numpy as jnp
from jax import lax
from jax.experimental import pallas as pl
from jax.experimental.pallas import tpu as pltpu
from jax.sharding import Mesh, PartitionSpec as P

beta_one = 0.95
beta_two = 0.95
epsilon = 1e-08
bias_one = 1.0 - 0.95**10
bias_two = 1.0 - 0.95**10

MP = ("y", "xh", "c")
DP = ("z", "xl")
F32 = jnp.float32
BF16 = jnp.bfloat16
VMEM = pl.BlockSpec(memory_space=pltpu.VMEM)
SMEM = pl.BlockSpec(memory_space=pltpu.SMEM)
PARAMS = pltpu.CompilerParams(vmem_limit_bytes=24 * 1024 * 1024)


def swap_groups(pieces):
    lane = lax.broadcasted_iota(jnp.int32, (64, 128), 1)
    pieces = list(pieces)
    for bit in (1, 2, 4):
        low = (lane // (16 * bit)) % 2 == 0
        for first in range(8):
            if first & bit:
                continue
            a, b = pieces[first], pieces[first | bit]
            pieces[first] = jnp.where(low, a, pltpu.roll(b, 16 * bit, 1))
            pieces[first | bit] = jnp.where(low, pltpu.roll(a, 128 - 16 * bit, 1), b)
    return pieces


def lane_tiles_to_rows(eight):
    return jnp.concatenate([eight[:, 128 * t : 128 * t + 128] for t in range(8)], axis=0)


def to_messages(pieces):
    swapped = [piece.reshape(8, 8, 128) for piece in swap_groups(pieces)]
    return jnp.stack(swapped, axis=1).reshape(512, 128).astype(BF16)


def from_messages(arrived, shift):
    wide = arrived.astype(F32)
    later = pltpu.roll(wide, 128 - shift, 1)
    rows = jnp.stack([wide.reshape(64, 8, 128), later.reshape(64, 8, 128)], axis=1)
    return rows.reshape(1024, 128).T


def turn_kernel(shares, moment, left, moment_out, message):
    turned = []
    for b in range(2):
        grad = shares[0, b].astype(F32)
        for r in range(1, 8):
            grad = grad + shares[r, b].astype(F32)
        new = beta_one * moment[b] + (1.0 - beta_one) * grad
        moment_out[b] = new
        both = jnp.concatenate([grad.astype(BF16), new.astype(BF16)], axis=0)
        turned.append(jnp.dot(both, left[b], preferred_element_type=F32))
    pieces = [
        lane_tiles_to_rows(turned[b][16 * x + 8 * half : 16 * x + 8 * half + 8])
        for half in range(2)
        for b in range(2)
        for x in range(2)
    ]
    message[...] = to_messages(pieces)


def step_kernel(arrived, second, right, second_out, message):
    turned = from_messages(arrived[...], 64)[:64].astype(BF16)
    returned = []
    for b in range(2):
        rotated = jnp.dot(turned[32 * b : 32 * b + 32], right[b], preferred_element_type=F32)
        grad, moment = rotated[:16], rotated[16:]
        new = beta_two * second[b] + (1.0 - beta_two) * grad * grad
        second_out[b] = new
        ratio = (moment / bias_one / (jnp.sqrt(new / bias_two) + epsilon)).astype(BF16)
        returned.append(
            lax.dot_general(ratio, right[b], (((1,), (1,)), ((), ())), preferred_element_type=F32)
        )
    pieces = [
        lane_tiles_to_rows(returned[b][8 * half : 8 * half + 8])
        for half in range(2)
        for b in range(2)
    ]
    message[...] = to_messages(pieces + [jnp.zeros((64, 128), F32)] * 4)


def back_kernel(scale, arrived, left, update):
    returned = from_messages(arrived[...], 32)[:32].astype(BF16)
    for b in range(2):
        step = lax.dot_general(
            returned[16 * b : 16 * b + 16],
            left[b],
            (((1,), (1,)), ((), ())),
            preferred_element_type=F32,
        )
        update[b] = scale[b] * step


def strips():
    return jax.ShapeDtypeStruct((2, 16, 1024), F32)


def messages():
    return jax.ShapeDtypeStruct((512, 128), BF16)


def cost(products, size):
    return pl.CostEstimate(flops=2 * products * 1024 * 1024, bytes_accessed=size, transcendentals=0)


def turn(shares, momentum, left):
    return pl.pallas_call(
        turn_kernel,
        out_shape=(strips(), messages()),
        in_specs=[VMEM] * 3,
        out_specs=(VMEM, VMEM),
        compiler_params=PARAMS,
        cost_estimate=cost(64, 5 << 20),
        name="turn",
    )(shares, momentum, left)


def step(arrived, second, right):
    return pl.pallas_call(
        step_kernel,
        out_shape=(strips(), messages()),
        in_specs=[VMEM] * 3,
        out_specs=(VMEM, VMEM),
        compiler_params=PARAMS,
        cost_estimate=cost(96, 5 << 20),
        name="step",
    )(arrived, second, right)


def back(scale, arrived, left):
    return pl.pallas_call(
        back_kernel,
        out_shape=strips(),
        in_specs=[SMEM, VMEM, VMEM],
        out_specs=VMEM,
        compiler_params=PARAMS,
        cost_estimate=cost(32, 5 << 20),
        name="back",
    )(scale, arrived, left)


def trade(message):
    return lax.all_to_all(message, MP, split_axis=0, concat_axis=0, tiled=True)


def local(grad_parts, momentum, second_moment, left_basis, right_basis, lr_scale):
    parts = grad_parts[0].reshape(8, 2, 2, 16, 1024)
    side = lax.axis_index("xl")
    away = lax.dynamic_index_in_dim(parts, 1 - side, 1, keepdims=False)
    kept = lax.dynamic_index_in_dim(parts, side, 1, keepdims=False)
    came = lax.ppermute(away, "xl", [(0, 1), (1, 0)])
    pair = (kept.astype(F32) + came.astype(F32)).astype(BF16)
    shares = lax.all_to_all(pair, "z", split_axis=0, concat_axis=0, tiled=True)
    momentum_out, message = turn(shares, momentum, left_basis)
    second_out, message = step(trade(message), second_moment, right_basis)
    update = back(lr_scale, trade(message), left_basis)
    return (update, momentum_out, second_out)


def solution(mesh):
    fine = Mesh(mesh.devices.reshape(8, 2, 8, 4, 2), DP + MP)
    in_specs = (
        P(DP, None, MP, None),
        P(DP, MP, None),
        P(DP, MP, None),
        P(DP, None, None),
        P(DP, None, None),
        P(DP),
    )
    out_specs = (P(DP, MP, None), P(DP, MP, None), P(DP, MP, None))
    return jax.shard_map(local, mesh=fine, in_specs=in_specs, out_specs=out_specs, check_vma=False)
```

time: 115 us -> 108 us (0.939)
  matrix products: 11.4 us -> 0 us
  Pallas kernels: 0 us -> 6.24 us
  local copies, waits for them, and re-layouts: 8.58 us -> 6.41 us
    dot_general x4 -> x0, matrix products: 11.4 us -> none  [the longest x1 4.05 us: local(): jnp.einsum('bik,bkj->bji', left_basis, landed, preferred_element_type=jnp...]
    pallas_call x0 -> x3, Pallas kernels: none -> 6.24 us  [the longest x1 2.47 us: back(): pl.pallas_call(back_kernel, out_shape=strips(), in_specs=[SMEM, VMEM, VME...]
    all_to_all x4 -> x0, local copies, waits for them, and re-layouts: 3.41 us -> none  [the longest x2 2.45 us: local(): lax.all_to_all(turned, MP, split_axis=2, concat_axis=3, tiled=True)]
    unnamed x14 -> x12, local copies, waits for them, and re-layouts: 2.92 us -> 5.29 us
where the time goes in v2:
time: 108 us
  blocking collectives  82 us (76%)
  waiting for transfers between devices  7.38 us (7%)
  local copies, waits for them, and re-layouts  6.41 us (6%)
  Pallas kernels  6.24 us (6%)
  starting transfers between devices  3.95 us (4%)
  other arithmetic  1.23 us (1%)
    all_to_all x2, blocking collectives, trade(): return lax.all_to_all(message, MP, split_axis=0, concat_axis=0, tiled=True)  46.8 us
    all_to_all x1, blocking collectives, local(): shares = lax.all_to_all(pair, 'z', split_axis=0, concat_axis=0, tiled=True)  35.1 us
    ppermute x1, waiting for transfers between devices, local(): came = lax.ppermute(away, 'xl', [(0, 1), (1, 0)])  7.38 us
    unnamed x12, local copies, waits for them, and re-layouts  5.29 us
    ppermute x1, starting transfers between devices, local(): came = lax.ppermute(away, 'xl', [(0, 1), (1, 0)])  3.95 us
    pallas_call x1, Pallas kernels, back(): pl.pallas_call(back_kernel, out_shape=strips(), in_specs=[SMEM, VMEM, VME...  2.47 us
    pallas_call x1, Pallas kernels, step(): pl.pallas_call(step_kernel, out_shape=(strips(), messages()), in_specs=[V...  2.29 us
  transfers between devices with their start and end apart: 1, of which 1 were waited for; matrix products, arithmetic and copies ran while one was open for 0% of the time, Pallas kernels for 0%

profile of v2, /device:TPU:1, one launch (start us, length us, event | category | flops | bytes accessed | tf_op | source)
XLA Modules:
  0.0 107.9 jit_solution(2640206750351783518)
XLA Ops:
  0.6 0.0 copy-start.4
  0.6 1.1 %dynamic-slice_bitcast_fusion = bf16[8,2,16,1024]{3,2,1,0:T(8,128)(2,1)S(1)} fusion(bf16[8,2,2,16,1024]{4,3,2,1,0:T(8,128)(2,1)} %bitcast.16, s32[]{:T(128)S(6)} %select_n.8), kind=kLoop, calls=%fused_computation.2 | loop fusion | bytes 1048580 | tf_op jit(solution)/shard_map/jit(dynamic_index_in_dim)/squeeze | solution.py:159
  1.8 3.9 %collective-permute-start = (bf16[8,2,16,1024]{3,2,1,0:T(8,128)(2,1)S(1)}, bf16[8,2,16,1024]{3,2,1,0:T(8,128)(2,1)S(1)}, u32[]{:S(2)}, u32[]{:S(2)}) collective-permute-start(bf16[8,2,16,1024]{3,2,1,0:T(8,128)(2,1)S(1)} %dynamic-slice_bitcast_fusion), channel_id=1, source_target_pairs={{0,64},{64,0},{1,65},{65,1},{2,66},{66,2},{3,67},{67,3},{4,68},{68... | collective-permute-start | bytes 1572872 | tf_op jit(solution)/shard_map/ppermute | solution.py:161
  5.7 7.4 %collective-permute-done = bf16[8,2,16,1024]{3,2,1,0:T(8,128)(2,1)S(1)} collective-permute-done((bf16[8,2,16,1024]{3,2,1,0:T(8,128)(2,1)S(1)}, bf16[8,2,16,1024]{3,2,1,0:T(8,128)(2,1)S(1)}, u32[]{:S(2)}, u32[]{:S(2)}) %collective-permute-start) | collective-permute-done | bytes 524320 | tf_op jit(solution)/shard_map/ppermute | solution.py:161
  13.1 1.2 %fusion = bf16[8,2,16,1024]{3,2,1,0:T(8,128)(2,1)S(1)} fusion(bf16[8,2,16,1024]{3,2,1,0:T(8,128)(2,1)S(1)} %collective-permute-done, bf16[8,2,2,16,1024]{4,3,2,1,0:T(8,128)(2,1)} %bitcast.17, s32[]{:T(128)S(6)} %select_n.7), kind=kLoop, calls=%fused_computation.1 | loop fusion | flops 1048576 | bytes 1572868 | tf_op jit(solution)/shard_map/convert_element_type | solution.py:162
  14.3 35.1 %all_to_all.27.shares = bf16[8,2,16,1024]{3,2,1,0:T(8,128)(2,1)S(1)} all-to-all(bf16[8,2,16,1024]{3,2,1,0:T(8,128)(2,1)S(1)} %fusion), channel_id=1, replica_groups=mesh['z'=8,'xl'=2,'y'=8,'xh'=4,'c'=2] {'z'}, dimensions={0} | all-to-all | bytes 1048576 | tf_op jit(solution)/shard_map/all_to_all | solution.py:163
  49.5 0.0 copy-start
  49.5 2.2 %copy-done = bf16[2,1024,1024]{2,1,0:T(8,128)(2,1)S(1)} copy-done((bf16[2,1024,1024]{2,1,0:T(8,128)(2,1)S(1)}, bf16[2,1024,1024]{2,1,0:T(8,128)(2,1)}, u32[]{:S(2)}) %copy-start) | copy-done | bytes 4194328
  51.7 0.0 copy-start.3
  51.7 0.9 copy-done.3
  52.6 0.0 copy-start.1
  52.6 0.0 copy-start.5
  52.6 1.5 %turn.1 = (f32[2,16,1024]{2,1,0:T(8,128)}, bf16[512,128]{1,0:T(8,128)(2,1)S(1)}) custom-call(bf16[8,2,16,1024]{3,2,1,0:T(8,128)(2,1)S(1)} %all_to_all.27.shares, f32[2,16,1024]{2,1,0:T(8,128)S(1)} %copy-done.3, bf16[2,1024,1024]{2,1,0:T(8,128)(2,1)S(1)} %copy-done), custom_call_target="tpu_custom_call" | custom-call | flops 134217728 | bytes 5242880 | tf_op jit(solution)/shard_map/turn/pallas_call | solution.py:117
  54.1 29.6 %all_to_all.28 = bf16[64,8,128]{2,1,0:T(8,128)(2,1)S(1)} all-to-all(bf16[64,8,128]{2,1,0:T(8,128)(2,1)S(1)} %bitcast.14), channel_id=1, replica_groups=mesh['z'=8,'xl'=2,'y'=8,'xh'=4,'c'=2] {'y','xh','c'}, dimensions={0} | all-to-all | bytes 262144 | tf_op jit(solution)/shard_map/all_to_all | solution.py:153
  83.7 0.0 copy-done.4
  83.7 0.0 copy-start.2
  83.7 2.2 %copy-done.2 = bf16[2,1024,1024]{2,1,0:T(8,128)(2,1)S(1)} copy-done((bf16[2,1024,1024]{2,1,0:T(8,128)(2,1)S(1)}, bf16[2,1024,1024]{2,1,0:T(8,128)(2,1)}, u32[]{:S(2)}) %copy-start.2) | copy-done | bytes 4194328
  85.9 2.3 %step.1 = (f32[2,16,1024]{2,1,0:T(8,128)}, bf16[512,128]{1,0:T(8,128)(2,1)S(1)}) custom-call(bf16[512,128]{1,0:T(8,128)(2,1)S(1)} %bitcast.12, f32[2,16,1024]{2,1,0:T(8,128)S(1)} %copy-done.4, bf16[2,1024,1024]{2,1,0:T(8,128)(2,1)S(1)} %copy-done.2), custom_call_target="tpu_custom_call" | custom-call | flops 201326592 | bytes 5242880 | tf_op jit(solution)/shard_map/step/pallas_call | solution.py:129
  88.2 17.2 %all_to_all.29 = bf16[64,8,128]{2,1,0:T(8,128)(2,1)S(1)} all-to-all(bf16[64,8,128]{2,1,0:T(8,128)(2,1)S(1)} %bitcast.15), channel_id=1, replica_groups=mesh['z'=8,'xl'=2,'y'=8,'xh'=4,'c'=2] {'y','xh','c'}, dimensions={0} | all-to-all | bytes 262144 | tf_op jit(solution)/shard_map/all_to_all | solution.py:153
  105.4 0.0 copy-done.1
  105.4 0.0 copy-done.5
  105.4 2.5 %back.1 = f32[2,16,1024]{2,1,0:T(8,128)} custom-call(f32[2]{0:T(128)S(1)} %copy-done.5, bf16[512,128]{1,0:T(8,128)(2,1)S(1)} %bitcast.13, bf16[2,1024,1024]{2,1,0:T(8,128)(2,1)S(1)} %copy-done.1), custom_call_target="tpu_custom_call" | custom-call | flops 67108864 | bytes 5242880 | tf_op jit(solution)/shard_map/back/pallas_call | solution.py:141
Async XLA Ops:
  0.6 83.1 %copy-start.4 = (f32[2,16,1024]{2,1,0:T(8,128)S(1)}, f32[2,16,1024]{2,1,0:T(8,128)}, u32[]{:S(2)}) copy-start(f32[2,16,1024]{2,1,0:T(8,128)} %second.1) | copy-start | bytes 393220
  1.8 11.3 %collective-permute-start = (bf16[8,2,16,1024]{3,2,1,0:T(8,128)(2,1)S(1)}, bf16[8,2,16,1024]{3,2,1,0:T(8,128)(2,1)S(1)}, u32[]{:S(2)}, u32[]{:S(2)}) collective-permute-start(bf16[8,2,16,1024]{3,2,1,0:T(8,128)(2,1)S(1)} %dynamic-slice_bitcast_fusion), channel_id=1, source_target_pairs={{0,64},{64,0},{1,65},{65,1},{2,66},{66,2},{3,67},{67,3},{4,68},{68... | collective-permute-start | bytes 1572872 | tf_op jit(solution)/shard_map/ppermute | solution.py:161
  49.5 2.2 %copy-start = (bf16[2,1024,1024]{2,1,0:T(8,128)(2,1)S(1)}, bf16[2,1024,1024]{2,1,0:T(8,128)(2,1)}, u32[]{:S(2)}) copy-start(bf16[2,1024,1024]{2,1,0:T(8,128)(2,1)} %left.3) | copy-start | bytes 12582916
  51.7 0.9 copy-start.3
  52.6 52.8 %copy-start.1 = (bf16[2,1024,1024]{2,1,0:T(8,128)(2,1)S(1)}, bf16[2,1024,1024]{2,1,0:T(8,128)(2,1)}, u32[]{:S(2)}) copy-start(bf16[2,1024,1024]{2,1,0:T(8,128)(2,1)} %left.3) | copy-start | bytes 12582916
  52.6 52.8 %copy-start.5 = (f32[2]{0:T(128)S(1)}, f32[2]{0:T(128)}, u32[]{:S(2)}) copy-start(f32[2]{0:T(128)} %scale.1) | copy-start | bytes 28
  83.7 2.2 %copy-start.2 = (bf16[2,1024,1024]{2,1,0:T(8,128)(2,1)S(1)}, bf16[2,1024,1024]{2,1,0:T(8,128)(2,1)}, u32[]{:S(2)}) copy-start(bf16[2,1024,1024]{2,1,0:T(8,128)(2,1)} %right.1) | copy-start | bytes 12582916

commit v3 on v2

--- a/solution.py
+++ b/solution.py
@@ -101,6 +101,24 @@
         update[b] = scale[b] * step
 
 
+def away_kernel(side, parts, away, sem):
+    copy = pltpu.make_async_copy(parts.at[:, 1 - side[0]], away, sem)
+    copy.start()
+    copy.wait()
+
+
+def hold_kernel(side, parts, left, right, kept, left_held, right_held, sems):
+    copies = [
+        pltpu.make_async_copy(parts.at[:, side[0]], kept, sems.at[0]),
+        pltpu.make_async_copy(left, left_held, sems.at[1]),
+        pltpu.make_async_copy(right, right_held, sems.at[2]),
+    ]
+    for copy in copies:
+        copy.start()
+    for copy in copies:
+        copy.wait()
+
+
 def strips():
     return jax.ShapeDtypeStruct((2, 16, 1024), F32)
 
@@ -111,6 +129,40 @@
 
 def cost(products, size):
     return pl.CostEstimate(flops=2 * products * 1024 * 1024, bytes_accessed=size, transcendentals=0)
+
+
+ANY = pl.BlockSpec(memory_space=pl.ANY)
+
+
+def half():
+    return jax.ShapeDtypeStruct((8, 2, 16, 1024), BF16)
+
+
+def take_away(side, parts):
+    return pl.pallas_call(
+        away_kernel,
+        out_shape=half(),
+        in_specs=[SMEM, ANY],
+        out_specs=ANY,
+        scratch_shapes=[pltpu.SemaphoreType.DMA],
+        compiler_params=PARAMS,
+        cost_estimate=cost(0, 1 << 20),
+        name="take_away",
+    )(side, parts)
+
+
+def hold(side, parts, left, right):
+    basis = jax.ShapeDtypeStruct((2, 1024, 1024), BF16)
+    return pl.pallas_call(
+        hold_kernel,
+        out_shape=(half(), basis, basis),
+        in_specs=[SMEM, ANY, ANY, ANY],
+        out_specs=(ANY, ANY, ANY),
+        scratch_shapes=[pltpu.SemaphoreType.DMA((3,))],
+        compiler_params=PARAMS,
+        cost_estimate=cost(0, 18 << 20),
+        name="hold",
+    )(side, parts, left, right)
 
 
 def turn(shares, momentum, left):
@@ -155,10 +207,10 @@
 
 def local(grad_parts, momentum, second_moment, left_basis, right_basis, lr_scale):
     parts = grad_parts[0].reshape(8, 2, 2, 16, 1024)
-    side = lax.axis_index("xl")
-    away = lax.dynamic_index_in_dim(parts, 1 - side, 1, keepdims=False)
-    kept = lax.dynamic_index_in_dim(parts, side, 1, keepdims=False)
+    side = lax.axis_index("xl").reshape(1)
+    away = take_away(side, parts)
     came = lax.ppermute(away, "xl", [(0, 1), (1, 0)])
+    kept, left_basis, right_basis = hold(side, parts, left_basis, right_basis)
     pair = (kept.astype(F32) + came.astype(F32)).astype(BF16)
     shares = lax.all_to_all(pair, "z", split_axis=0, concat_axis=0, tiled=True)
     momentum_out, message = turn(shares, momentum, left_basis)

time: 108 us -> 102 us (0.944)
  waiting for transfers between devices: 7.38 us -> 2.36 us
    ppermute x1, waiting for transfers between devices: 7.38 us -> 2.36 us  [local(): came = lax.ppermute(away, 'xl', [(0, 1), (1, 0)])]
    squeeze x1 -> x0, local copies, waits for them, and re-layouts: 1.12 us -> none  [local(): away = lax.dynamic_index_in_dim(parts, 1 - side, 1, keepdims=False)]
  transfers between devices with their start and end apart: 1 -> 1, of which waited for: 1 -> 1; matrix products, arithmetic and copies ran while one was open for 0% -> 0% of each run, Pallas kernels for 0% -> 1%
where the time goes in v3:
time: 102 us
  blocking collectives  82 us (80%)
  Pallas kernels  6.94 us (7%)
  local copies, waits for them, and re-layouts  5.6 us (5%)
  starting transfers between devices  3.95 us (4%)
  waiting for transfers between devices  2.36 us (2%)
    all_to_all x2, blocking collectives, trade(): return lax.all_to_all(message, MP, split_axis=0, concat_axis=0, tiled=True)  46.9 us
    all_to_all x1, blocking collectives, local(): shares = lax.all_to_all(pair, 'z', split_axis=0, concat_axis=0, tiled=True)  35.1 us
    unnamed x12, local copies, waits for them, and re-layouts  5.6 us
    ppermute x1, starting transfers between devices, local(): came = lax.ppermute(away, 'xl', [(0, 1), (1, 0)])  3.95 us
    pallas_call x1, Pallas kernels, back(): pl.pallas_call(back_kernel, out_shape=strips(), in_specs=[SMEM, VMEM, VME...  2.47 us
    ppermute x1, waiting for transfers between devices, local(): came = lax.ppermute(away, 'xl', [(0, 1), (1, 0)])  2.36 us
    pallas_call x1, Pallas kernels, step(): pl.pallas_call(step_kernel, out_shape=(strips(), messages()), in_specs=[V...  2.29 us
  transfers between devices with their start and end apart: 1, of which 1 were waited for; matrix products, arithmetic and copies ran while one was open for 0% of the time, Pallas kernels for 1%

profile of v3, /device:TPU:1, one launch (start us, length us, event | category | flops | bytes accessed | tf_op | source)
XLA Modules:
  0.0 101.7 jit_solution(16048912965267277427)
XLA Ops:
  0.6 0.0 copy-start.2
  0.6 1.2 %copy-done.2 = bf16[1,32,16,1024]{3,2,1,0:T(8,128)(2,1)S(1)} copy-done((bf16[1,32,16,1024]{3,2,1,0:T(8,128)(2,1)S(1)}, bf16[1,32,16,1024]{3,2,1,0:T(8,128)(2,1)}, u32[]{:S(2)}) %copy-start.2) | copy-done | bytes 1048600
  1.9 3.9 %collective-permute-start = (bf16[8,2,16,1024]{3,2,1,0:T(8,128)(2,1)S(1)}, bf16[8,2,16,1024]{3,2,1,0:T(8,128)(2,1)S(1)}, u32[]{:S(2)}, u32[]{:S(2)}) collective-permute-start(bf16[8,2,16,1024]{3,2,1,0:T(8,128)(2,1)S(1)} %take_away.1), channel_id=1, source_target_pairs={{0,64},{64,0},{1,65},{65,1},{2,66},{66,2},{3,67},{67,3},{4,68},{68... | collective-permute-start | bytes 1572872 | tf_op jit(solution)/shard_map/ppermute | solution.py:212
  5.9 0.0 copy-start
  5.9 2.2 %copy-done = bf16[2,1024,1024]{2,1,0:T(8,128)(2,1)S(1)} copy-done((bf16[2,1024,1024]{2,1,0:T(8,128)(2,1)S(1)}, bf16[2,1024,1024]{2,1,0:T(8,128)(2,1)}, u32[]{:S(2)}) %copy-start) | copy-done | bytes 4194328
  8.1 0.0 copy-start.1
  8.1 2.2 %copy-done.1 = bf16[2,1024,1024]{2,1,0:T(8,128)(2,1)S(1)} copy-done((bf16[2,1024,1024]{2,1,0:T(8,128)(2,1)S(1)}, bf16[2,1024,1024]{2,1,0:T(8,128)(2,1)}, u32[]{:S(2)}) %copy-start.1) | copy-done | bytes 4194328
  10.2 0.0 copy-start.3
  10.3 0.6 hold.1
  10.9 0.0 copy-start.4
  10.9 2.4 %collective-permute-done = bf16[8,2,16,1024]{3,2,1,0:T(8,128)(2,1)S(1)} collective-permute-done((bf16[8,2,16,1024]{3,2,1,0:T(8,128)(2,1)S(1)}, bf16[8,2,16,1024]{3,2,1,0:T(8,128)(2,1)S(1)}, u32[]{:S(2)}, u32[]{:S(2)}) %collective-permute-start) | collective-permute-done | bytes 524320 | tf_op jit(solution)/shard_map/ppermute | solution.py:212
  13.3 0.2 add_convert_fusion
  13.5 35.1 %all_to_all.27.shares = bf16[8,2,16,1024]{3,2,1,0:T(8,128)(2,1)S(1)} all-to-all(bf16[8,2,16,1024]{3,2,1,0:T(8,128)(2,1)S(1)} %add_convert_fusion), channel_id=1, replica_groups=mesh['z'=8,'xl'=2,'y'=8,'xh'=4,'c'=2] {'z'}, dimensions={0} | all-to-all | bytes 1048576 | tf_op jit(solution)/shard_map/all_to_all | solution.py:215
  48.6 0.0 copy-done.3
  48.6 0.0 copy-start.5
  48.6 1.5 %turn.1 = (f32[2,16,1024]{2,1,0:T(8,128)}, bf16[512,128]{1,0:T(8,128)(2,1)S(1)}) custom-call(bf16[8,2,16,1024]{3,2,1,0:T(8,128)(2,1)S(1)} %all_to_all.27.shares, f32[2,16,1024]{2,1,0:T(8,128)S(1)} %copy-done.3, bf16[2,1024,1024]{2,1,0:T(8,128)(2,1)S(1)} %get-tuple-element.11.left), custom_call_target="tpu_custom_call" | custom-call | flops 134217728 | bytes 5242880 | tf_op jit(solution)/shard_map/turn/pallas_call | solution.py:169
  50.1 29.7 %all_to_all.28 = bf16[64,8,128]{2,1,0:T(8,128)(2,1)S(1)} all-to-all(bf16[64,8,128]{2,1,0:T(8,128)(2,1)S(1)} %bitcast.11), channel_id=1, replica_groups=mesh['z'=8,'xl'=2,'y'=8,'xh'=4,'c'=2] {'y','xh','c'}, dimensions={0} | all-to-all | bytes 262144 | tf_op jit(solution)/shard_map/all_to_all | solution.py:205
  79.8 0.0 copy-done.4
  79.8 2.3 %step.1 = (f32[2,16,1024]{2,1,0:T(8,128)}, bf16[512,128]{1,0:T(8,128)(2,1)S(1)}) custom-call(bf16[512,128]{1,0:T(8,128)(2,1)S(1)} %bitcast.8, f32[2,16,1024]{2,1,0:T(8,128)S(1)} %copy-done.4, bf16[2,1024,1024]{2,1,0:T(8,128)(2,1)S(1)} %get-tuple-element.13.right), custom_call_target="tpu_custom_call" | custom-call | flops 201326592 | bytes 5242880 | tf_op jit(solution)/shard_map/step/pallas_call | solution.py:181
  82.1 17.2 %all_to_all.29 = bf16[64,8,128]{2,1,0:T(8,128)(2,1)S(1)} all-to-all(bf16[64,8,128]{2,1,0:T(8,128)(2,1)S(1)} %bitcast.10), channel_id=1, replica_groups=mesh['z'=8,'xl'=2,'y'=8,'xh'=4,'c'=2] {'y','xh','c'}, dimensions={0} | all-to-all | bytes 262144 | tf_op jit(solution)/shard_map/all_to_all | solution.py:205
  99.3 0.0 copy-done.5
  99.3 2.5 %back.1 = f32[2,16,1024]{2,1,0:T(8,128)} custom-call(f32[2]{0:T(128)S(1)} %copy-done.5, bf16[512,128]{1,0:T(8,128)(2,1)S(1)} %bitcast.9, bf16[2,1024,1024]{2,1,0:T(8,128)(2,1)S(1)} %get-tuple-element.11.left), custom_call_target="tpu_custom_call" | custom-call | flops 67108864 | bytes 5242880 | tf_op jit(solution)/shard_map/back/pallas_call | solution.py:193
  (1 shorter events, 0.0 us)
Async XLA Ops:
  0.6 1.2 %copy-start.2 = (bf16[1,32,16,1024]{3,2,1,0:T(8,128)(2,1)S(1)}, bf16[1,32,16,1024]{3,2,1,0:T(8,128)(2,1)}, u32[]{:S(2)}) copy-start(bf16[1,32,16,1024]{3,2,1,0:T(8,128)(2,1)} %param.6) | copy-start | bytes 3145732
  1.9 11.3 %collective-permute-start = (bf16[8,2,16,1024]{3,2,1,0:T(8,128)(2,1)S(1)}, bf16[8,2,16,1024]{3,2,1,0:T(8,128)(2,1)S(1)}, u32[]{:S(2)}, u32[]{:S(2)}) collective-permute-start(bf16[8,2,16,1024]{3,2,1,0:T(8,128)(2,1)S(1)} %take_away.1), channel_id=1, source_target_pairs={{0,64},{64,0},{1,65},{65,1},{2,66},{66,2},{3,67},{67,3},{4,68},{68... | collective-permute-start | bytes 1572872 | tf_op jit(solution)/shard_map/ppermute | solution.py:212
  5.9 2.2 %copy-start = (bf16[2,1024,1024]{2,1,0:T(8,128)(2,1)S(1)}, bf16[2,1024,1024]{2,1,0:T(8,128)(2,1)}, u32[]{:S(2)}) copy-start(bf16[2,1024,1024]{2,1,0:T(8,128)(2,1)} %left.1) | copy-start | bytes 12582916
  8.1 2.2 %copy-start.1 = (bf16[2,1024,1024]{2,1,0:T(8,128)(2,1)S(1)}, bf16[2,1024,1024]{2,1,0:T(8,128)(2,1)}, u32[]{:S(2)}) copy-start(bf16[2,1024,1024]{2,1,0:T(8,128)(2,1)} %right.1) | copy-start | bytes 12582916
  10.2 38.3 %copy-start.3 = (f32[2,16,1024]{2,1,0:T(8,128)S(1)}, f32[2,16,1024]{2,1,0:T(8,128)}, u32[]{:S(2)}) copy-start(f32[2,16,1024]{2,1,0:T(8,128)} %moment.1) | copy-start | bytes 393220
  10.9 68.9 %copy-start.4 = (f32[2,16,1024]{2,1,0:T(8,128)S(1)}, f32[2,16,1024]{2,1,0:T(8,128)}, u32[]{:S(2)}) copy-start(f32[2,16,1024]{2,1,0:T(8,128)} %second.1) | copy-start | bytes 393220
  48.6 50.7 %copy-start.5 = (f32[2]{0:T(128)S(1)}, f32[2]{0:T(128)}, u32[]{:S(2)}) copy-start(f32[2]{0:T(128)} %scale.1) | copy-start | bytes 28

commit v4 on v3

--- a/solution.py
+++ b/solution.py
@@ -69,7 +69,7 @@
     message[...] = to_messages(pieces)
 
 
-def step_kernel(arrived, second, right, second_out, message):
+def step_kernel(arrived, second, right, right_turned, second_out, message):
     turned = from_messages(arrived[...], 64)[:64].astype(BF16)
     returned = []
     for b in range(2):
@@ -79,7 +79,7 @@
         second_out[b] = new
         ratio = (moment / bias_one / (jnp.sqrt(new / bias_two) + epsilon)).astype(BF16)
         returned.append(
-            lax.dot_general(ratio, right[b], (((1,), (1,)), ((), ())), preferred_element_type=F32)
+            jnp.dot(ratio, right_turned[b], preferred_element_type=F32)
         )
     pieces = [
         lane_tiles_to_rows(returned[b][8 * half : 8 * half + 8])
@@ -89,16 +89,16 @@
     message[...] = to_messages(pieces + [jnp.zeros((64, 128), F32)] * 4)
 
 
-def back_kernel(scale, arrived, left, update):
+def back_kernel(scale, arrived, left, update, fresh, sems):
+    writes = []
     returned = from_messages(arrived[...], 32)[:32].astype(BF16)
     for b in range(2):
-        step = lax.dot_general(
-            returned[16 * b : 16 * b + 16],
-            left[b],
-            (((1,), (1,)), ((), ())),
-            preferred_element_type=F32,
-        )
-        update[b] = scale[b] * step
+        step = jnp.dot(returned[16 * b : 16 * b + 16], left[b], preferred_element_type=F32)
+        fresh[b] = scale[b][:, :1] * step
+        writes.append(pltpu.make_async_copy(fresh.at[b], update.at[b], sems.at[b]))
+        writes[b].start()
+    for write in writes:
+        write.wait()
 
 
 def away_kernel(side, parts, away, sem):
@@ -107,7 +107,9 @@
     copy.wait()
 
 
-def hold_kernel(side, parts, left, right, kept, left_held, right_held, sems):
+def hold_kernel(
+    side, parts, left, right, kept, left_held, right_held, right_turned, left_turned, sems
+):
     copies = [
         pltpu.make_async_copy(parts.at[:, side[0]], kept, sems.at[0]),
         pltpu.make_async_copy(left, left_held, sems.at[1]),
@@ -115,6 +117,9 @@
     ]
     for copy in copies:
         copy.start()
+    for b in range(2):
+        left_turned[b] = left[b].T
+        right_turned[b] = right[b].T
     for copy in copies:
         copy.wait()
 
@@ -131,6 +136,8 @@
     return pl.CostEstimate(flops=2 * products * 1024 * 1024, bytes_accessed=size, transcendentals=0)
 
 
+FRESH = [pltpu.VMEM((2, 16, 1024), F32), pltpu.SemaphoreType.DMA((2,))]
+HBM = pl.BlockSpec(memory_space=pltpu.HBM)
 ANY = pl.BlockSpec(memory_space=pl.ANY)
 
 
@@ -142,7 +149,7 @@
     return pl.pallas_call(
         away_kernel,
         out_shape=half(),
-        in_specs=[SMEM, ANY],
+        in_specs=[SMEM, HBM],
         out_specs=ANY,
         scratch_shapes=[pltpu.SemaphoreType.DMA],
         compiler_params=PARAMS,
@@ -155,9 +162,9 @@
     basis = jax.ShapeDtypeStruct((2, 1024, 1024), BF16)
     return pl.pallas_call(
         hold_kernel,
-        out_shape=(half(), basis, basis),
-        in_specs=[SMEM, ANY, ANY, ANY],
-        out_specs=(ANY, ANY, ANY),
+        out_shape=(half(), basis, basis, basis, basis),
+        in_specs=[SMEM, HBM, VMEM, VMEM],
+        out_specs=(ANY, ANY, ANY, VMEM, VMEM),
         scratch_shapes=[pltpu.SemaphoreType.DMA((3,))],
         compiler_params=PARAMS,
         cost_estimate=cost(0, 18 << 20),
@@ -177,28 +184,33 @@
     )(shares, momentum, left)
 
 
-def step(arrived, second, right):
+def step(arrived, second, right, right_turned):
     return pl.pallas_call(
         step_kernel,
         out_shape=(strips(), messages()),
-        in_specs=[VMEM] * 3,
+        in_specs=[VMEM] * 4,
         out_specs=(VMEM, VMEM),
         compiler_params=PARAMS,
         cost_estimate=cost(96, 5 << 20),
         name="step",
-    )(arrived, second, right)
+    )(arrived, second, right, right_turned)
 
 
 def back(scale, arrived, left):
     return pl.pallas_call(
         back_kernel,
         out_shape=strips(),
-        in_specs=[SMEM, VMEM, VMEM],
-        out_specs=VMEM,
+        in_specs=[VMEM, VMEM, VMEM],
+        out_specs=ANY,
+        scratch_shapes=FRESH,
         compiler_params=PARAMS,
         cost_estimate=cost(32, 5 << 20),
         name="back",
     )(scale, arrived, left)
+
+
+def spread(scale):
+    return jnp.broadcast_to(scale[:, None, None], (2, 16, 128))
 
 
 def trade(message):
@@ -210,12 +222,12 @@
     side = lax.axis_index("xl").reshape(1)
     away = take_away(side, parts)
     came = lax.ppermute(away, "xl", [(0, 1), (1, 0)])
-    kept, left_basis, right_basis = hold(side, parts, left_basis, right_basis)
+    kept, left, right, right_turned, left_turned = hold(side, parts, left_basis, right_basis)
     pair = (kept.astype(F32) + came.astype(F32)).astype(BF16)
     shares = lax.all_to_all(pair, "z", split_axis=0, concat_axis=0, tiled=True)
-    momentum_out, message = turn(shares, momentum, left_basis)
-    second_out, message = step(trade(message), second_moment, right_basis)
-    update = back(lr_scale, trade(message), left_basis)
+    momentum_out, message = turn(shares, momentum, left)
+    second_out, message = step(trade(message), second_moment, right, right_turned)
+    update = back(spread(lr_scale), trade(message), left_turned)
     return (update, momentum_out, second_out)
 
 

time: 102 us -> 101 us (level)
  waiting for transfers between devices: 2.36 us -> 0.01 us
    ppermute x1, waiting for transfers between devices: 2.36 us -> 0.01 us  [local(): came = lax.ppermute(away, 'xl', [(0, 1), (1, 0)])]
    pallas_call x3, Pallas kernels: 3.14 us -> 4.51 us  [the longest x1 3.04 us: hold(): pl.pallas_call(hold_kernel, out_shape=(half(), basis, basis, basis, basis...]
  transfers between devices with their start and end apart: 1 -> 1, of which waited for: 1 -> 0; matrix products, arithmetic and copies ran while one was open for 0% -> 0% of each run, Pallas kernels for 1% -> 3%
where the time goes in v4:
time: 101 us; the launch traced here: 100 us
  blocking collectives  81.9 us (81%)
  Pallas kernels  7.94 us (8%)
  local copies, waits for them, and re-layouts  5.67 us (6%)
  starting transfers between devices  3.95 us (4%)
    all_to_all x2, blocking collectives, trade(): return lax.all_to_all(message, MP, split_axis=0, concat_axis=0, tiled=True)  46.8 us
    all_to_all x1, blocking collectives, local(): shares = lax.all_to_all(pair, 'z', split_axis=0, concat_axis=0, tiled=True)  35.1 us
    unnamed x12, local copies, waits for them, and re-layouts  5.6 us
    ppermute x1, starting transfers between devices, local(): came = lax.ppermute(away, 'xl', [(0, 1), (1, 0)])  3.95 us
    pallas_call x1, Pallas kernels, hold(): pl.pallas_call(hold_kernel, out_shape=(half(), basis, basis, basis, basis...  3.04 us
  transfers between devices with their start and end apart: 1, of which 0 were waited for; matrix products, arithmetic and copies ran while one was open for 0% of the time, Pallas kernels for 3%

profile of v4, /device:TPU:1, one launch (start us, length us, event | category | flops | bytes accessed | tf_op | source)
XLA Modules:
  0.0 100.4 jit_solution(9702936880680271073)
XLA Ops:
  0.6 0.0 copy-start.2
  0.6 1.2 %copy-done.2 = bf16[1,32,16,1024]{3,2,1,0:T(8,128)(2,1)S(1)} copy-done((bf16[1,32,16,1024]{3,2,1,0:T(8,128)(2,1)S(1)}, bf16[1,32,16,1024]{3,2,1,0:T(8,128)(2,1)}, u32[]{:S(2)}) %copy-start.2) | copy-done | bytes 1048600
  1.9 3.9 %collective-permute-start = (bf16[8,2,16,1024]{3,2,1,0:T(8,128)(2,1)S(1)}, bf16[8,2,16,1024]{3,2,1,0:T(8,128)(2,1)S(1)}, u32[]{:S(2)}, u32[]{:S(2)}) collective-permute-start(bf16[8,2,16,1024]{3,2,1,0:T(8,128)(2,1)S(1)} %take_away.1), channel_id=1, source_target_pairs={{0,64},{64,0},{1,65},{65,1},{2,66},{66,2},{3,67},{67,3},{4,68},{68... | collective-permute-start | bytes 1572872 | tf_op jit(solution)/shard_map/ppermute | solution.py:224
  5.9 0.0 copy-start
  5.9 2.2 %copy-done = bf16[2,1024,1024]{2,1,0:T(8,128)(2,1)S(1)} copy-done((bf16[2,1024,1024]{2,1,0:T(8,128)(2,1)S(1)}, bf16[2,1024,1024]{2,1,0:T(8,128)(2,1)}, u32[]{:S(2)}) %copy-start) | copy-done | bytes 4194328
  8.1 0.0 copy-start.1
  8.1 2.2 %copy-done.1 = bf16[2,1024,1024]{2,1,0:T(8,128)(2,1)S(1)} copy-done((bf16[2,1024,1024]{2,1,0:T(8,128)(2,1)S(1)}, bf16[2,1024,1024]{2,1,0:T(8,128)(2,1)}, u32[]{:S(2)}) %copy-start.1) | copy-done | bytes 4194328
  10.2 0.0 copy-start.4
  10.3 3.0 %hold.1 = (bf16[8,2,16,1024]{3,2,1,0:T(8,128)(2,1)S(1)}, bf16[2,1024,1024]{2,1,0:T(8,128)(2,1)S(1)}, bf16[2,1024,1024]{2,1,0:T(8,128)(2,1)S(1)}, bf16[2,1024,102...) custom-call(s32[1]{0:T(128)} %bitcast.side, bf16[8,2,2,16,1024]{4,3,2,1,0:T(8,128)(2,1)S(1)} %bitcast.7, ...), custom_call_target="tpu_custom_call" | custom-call | bytes 18874368 | tf_op jit(solution)/shard_map/hold/pallas_call | solution.py:163
  13.3 0.0 copy-start.3
  13.3 0.0 collective-permute-done
  13.3 0.2 add_convert_fusion
  13.5 35.1 %all_to_all.27.shares = bf16[8,2,16,1024]{3,2,1,0:T(8,128)(2,1)S(1)} all-to-all(bf16[8,2,16,1024]{3,2,1,0:T(8,128)(2,1)S(1)} %add_convert_fusion), channel_id=1, replica_groups=mesh['z'=8,'xl'=2,'y'=8,'xh'=4,'c'=2] {'z'}, dimensions={0} | all-to-all | bytes 1048576 | tf_op jit(solution)/shard_map/all_to_all | solution.py:227
  48.6 0.0 copy-done.4
  48.6 1.5 %turn.1 = (f32[2,16,1024]{2,1,0:T(8,128)}, bf16[512,128]{1,0:T(8,128)(2,1)S(1)}) custom-call(bf16[8,2,16,1024]{3,2,1,0:T(8,128)(2,1)S(1)} %all_to_all.27.shares, f32[2,16,1024]{2,1,0:T(8,128)S(1)} %copy-done.4, bf16[2,1024,1024]{2,1,0:T(8,128)(2,1)S(1)} %get-tuple-element.13.left), custom_call_target="tpu_custom_call" | custom-call | flops 134217728 | bytes 5242880 | tf_op jit(solution)/shard_map/turn/pallas_call | solution.py:176
  50.1 29.7 %all_to_all.28 = bf16[64,8,128]{2,1,0:T(8,128)(2,1)S(1)} all-to-all(bf16[64,8,128]{2,1,0:T(8,128)(2,1)S(1)} %bitcast.11), channel_id=1, replica_groups=mesh['z'=8,'xl'=2,'y'=8,'xh'=4,'c'=2] {'y','xh','c'}, dimensions={0} | all-to-all | bytes 262144 | tf_op jit(solution)/shard_map/all_to_all | solution.py:217
  79.7 0.0 copy-done.3
  79.7 0.0 copy-start.5
  79.8 1.9 %step.1 = (f32[2,16,1024]{2,1,0:T(8,128)}, bf16[512,128]{1,0:T(8,128)(2,1)S(1)}) custom-call(bf16[512,128]{1,0:T(8,128)(2,1)S(1)} %bitcast.8, f32[2,16,1024]{2,1,0:T(8,128)S(1)} %copy-done.3, bf16[2,1024,1024]{2,1,0:T(8,128)(2,1)S(1)} %get-tuple-element.15.right, bf16[2,1024,1024]{2,1,0:T(8,128)(2,1)S(1)} %get-tuple-element.16.right_turned), custom_call_target="tpu_custom_call" | custom-call | flops 201326592 | bytes 5242880 | tf_op jit(solution)/shard_map/step/pallas_call | solution.py:188
  81.7 17.2 %all_to_all.29 = bf16[64,8,128]{2,1,0:T(8,128)(2,1)S(1)} all-to-all(bf16[64,8,128]{2,1,0:T(8,128)(2,1)S(1)} %bitcast.10), channel_id=1, replica_groups=mesh['z'=8,'xl'=2,'y'=8,'xh'=4,'c'=2] {'y','xh','c'}, dimensions={0} | all-to-all | bytes 262144 | tf_op jit(solution)/shard_map/all_to_all | solution.py:217
  98.9 0.0 copy-done.5
  98.9 0.1 broadcast_in_dim.2.scale
  98.9 1.4 %back.1 = f32[2,16,1024]{2,1,0:T(8,128)} custom-call(f32[2,16,128]{2,1,0:T(8,128)S(1)} %broadcast_in_dim.2.scale, bf16[512,128]{1,0:T(8,128)(2,1)S(1)} %bitcast.9, bf16[2,1024,1024]{2,1,0:T(8,128)(2,1)S(1)} %get-tuple-element.18.left), custom_call_target="tpu_custom_call" | custom-call | flops 67108864 | bytes 5242880 | tf_op jit(solution)/shard_map/back/pallas_call | solution.py:200
  (1 shorter events, 0.0 us)
Async XLA Ops:
  0.6 1.2 %copy-start.2 = (bf16[1,32,16,1024]{3,2,1,0:T(8,128)(2,1)S(1)}, bf16[1,32,16,1024]{3,2,1,0:T(8,128)(2,1)}, u32[]{:S(2)}) copy-start(bf16[1,32,16,1024]{3,2,1,0:T(8,128)(2,1)} %param.6) | copy-start | bytes 3145732
  1.9 11.4 %collective-permute-start = (bf16[8,2,16,1024]{3,2,1,0:T(8,128)(2,1)S(1)}, bf16[8,2,16,1024]{3,2,1,0:T(8,128)(2,1)S(1)}, u32[]{:S(2)}, u32[]{:S(2)}) collective-permute-start(bf16[8,2,16,1024]{3,2,1,0:T(8,128)(2,1)S(1)} %take_away.1), channel_id=1, source_target_pairs={{0,64},{64,0},{1,65},{65,1},{2,66},{66,2},{3,67},{67,3},{4,68},{68... | collective-permute-start | bytes 1572872 | tf_op jit(solution)/shard_map/ppermute | solution.py:224
  5.9 2.2 %copy-start = (bf16[2,1024,1024]{2,1,0:T(8,128)(2,1)S(1)}, bf16[2,1024,1024]{2,1,0:T(8,128)(2,1)}, u32[]{:S(2)}) copy-start(bf16[2,1024,1024]{2,1,0:T(8,128)(2,1)} %left.1) | copy-start | bytes 12582916
  8.1 2.2 %copy-start.1 = (bf16[2,1024,1024]{2,1,0:T(8,128)(2,1)S(1)}, bf16[2,1024,1024]{2,1,0:T(8,128)(2,1)}, u32[]{:S(2)}) copy-start(bf16[2,1024,1024]{2,1,0:T(8,128)(2,1)} %right.1) | copy-start | bytes 12582916
  10.2 38.3 %copy-start.4 = (f32[2,16,1024]{2,1,0:T(8,128)S(1)}, f32[2,16,1024]{2,1,0:T(8,128)}, u32[]{:S(2)}) copy-start(f32[2,16,1024]{2,1,0:T(8,128)} %moment.1) | copy-start | bytes 393220
  13.3 66.5 %copy-start.3 = (f32[2,16,1024]{2,1,0:T(8,128)S(1)}, f32[2,16,1024]{2,1,0:T(8,128)}, u32[]{:S(2)}) copy-start(f32[2,16,1024]{2,1,0:T(8,128)} %second.1) | copy-start | bytes 393220
  79.7 19.1 %copy-start.5 = (f32[2]{0:T(128)S(1)}, f32[2]{0:T(128)}, u32[]{:S(2)}) copy-start(f32[2]{0:T(128)} %param.11) | copy-start | bytes 28

commit v5 on v4

--- a/solution.py
+++ b/solution.py
@@ -50,16 +50,16 @@
     return rows.reshape(1024, 128).T
 
 
-def turn_kernel(shares, moment, left, moment_out, message):
-    turned = []
+def turn_kernel(shares, moment, left, moment_new, message):
+    rows = []
     for b in range(2):
         grad = shares[0, b].astype(F32)
         for r in range(1, 8):
             grad = grad + shares[r, b].astype(F32)
         new = beta_one * moment[b] + (1.0 - beta_one) * grad
-        moment_out[b] = new
-        both = jnp.concatenate([grad.astype(BF16), new.astype(BF16)], axis=0)
-        turned.append(jnp.dot(both, left[b], preferred_element_type=F32))
+        moment_new[b] = new
+        rows.append(jnp.concatenate([grad.astype(BF16), new.astype(BF16)], axis=0))
+    turned = [jnp.dot(rows[b], left[b], preferred_element_type=F32) for b in range(2)]
     pieces = [
         lane_tiles_to_rows(turned[b][16 * x + 8 * half : 16 * x + 8 * half + 8])
         for half in range(2)
@@ -69,18 +69,17 @@
     message[...] = to_messages(pieces)
 
 
-def step_kernel(arrived, second, right, right_turned, second_out, message):
+def step_kernel(arrived, second, right, right_turned, second_new, message):
     turned = from_messages(arrived[...], 64)[:64].astype(BF16)
-    returned = []
+    ratios = []
     for b in range(2):
         rotated = jnp.dot(turned[32 * b : 32 * b + 32], right[b], preferred_element_type=F32)
         grad, moment = rotated[:16], rotated[16:]
         new = beta_two * second[b] + (1.0 - beta_two) * grad * grad
-        second_out[b] = new
+        second_new[b] = new
         ratio = (moment / bias_one / (jnp.sqrt(new / bias_two) + epsilon)).astype(BF16)
-        returned.append(
-            jnp.dot(ratio, right_turned[b], preferred_element_type=F32)
-        )
+        ratios.append(ratio)
+    returned = [jnp.dot(ratios[b], right_turned[b], preferred_element_type=F32) for b in range(2)]
     pieces = [
         lane_tiles_to_rows(returned[b][8 * half : 8 * half + 8])
         for half in range(2)
@@ -89,14 +88,21 @@
     message[...] = to_messages(pieces + [jnp.zeros((64, 128), F32)] * 4)
 
 
-def back_kernel(scale, arrived, left, update, fresh, sems):
-    writes = []
+def back_kernel(
+    scale, arrived, left, moment_new, second_new, update, moment_out, second_out, fresh, sems
+):
+    writes = [
+        pltpu.make_async_copy(moment_new, moment_out, sems.at[2]),
+        pltpu.make_async_copy(second_new, second_out, sems.at[3]),
+    ]
+    for write in writes:
+        write.start()
     returned = from_messages(arrived[...], 32)[:32].astype(BF16)
     for b in range(2):
         step = jnp.dot(returned[16 * b : 16 * b + 16], left[b], preferred_element_type=F32)
         fresh[b] = scale[b][:, :1] * step
         writes.append(pltpu.make_async_copy(fresh.at[b], update.at[b], sems.at[b]))
-        writes[b].start()
+        writes[-1].start()
     for write in writes:
         write.wait()
 
@@ -108,7 +114,18 @@
 
 
 def hold_kernel(
-    side, parts, left, right, kept, left_held, right_held, right_turned, left_turned, sems
+    side,
+    scale,
+    parts,
+    left,
+    right,
+    kept,
+    left_held,
+    right_held,
+    right_turned,
+    left_turned,
+    scale_rows,
+    sems,
 ):
     copies = [
         pltpu.make_async_copy(parts.at[:, side[0]], kept, sems.at[0]),
@@ -118,6 +135,7 @@
     for copy in copies:
         copy.start()
     for b in range(2):
+        scale_rows[b] = jnp.full((16, 128), scale[b], F32)
         left_turned[b] = left[b].T
         right_turned[b] = right[b].T
     for copy in copies:
@@ -136,7 +154,7 @@
     return pl.CostEstimate(flops=2 * products * 1024 * 1024, bytes_accessed=size, transcendentals=0)
 
 
-FRESH = [pltpu.VMEM((2, 16, 1024), F32), pltpu.SemaphoreType.DMA((2,))]
+FRESH = [pltpu.VMEM((2, 16, 1024), F32), pltpu.SemaphoreType.DMA((4,))]
 HBM = pl.BlockSpec(memory_space=pltpu.HBM)
 ANY = pl.BlockSpec(memory_space=pl.ANY)
 
@@ -158,18 +176,18 @@
     )(side, parts)
 
 
-def hold(side, parts, left, right):
+def hold(side, scale, parts, left, right):
     basis = jax.ShapeDtypeStruct((2, 1024, 1024), BF16)
     return pl.pallas_call(
         hold_kernel,
-        out_shape=(half(), basis, basis, basis, basis),
-        in_specs=[SMEM, HBM, VMEM, VMEM],
-        out_specs=(ANY, ANY, ANY, VMEM, VMEM),
+        out_shape=(half(), basis, basis, basis, basis, jax.ShapeDtypeStruct((2, 16, 128), F32)),
+        in_specs=[SMEM, SMEM, HBM, VMEM, VMEM],
+        out_specs=(ANY, ANY, ANY, VMEM, VMEM, VMEM),
         scratch_shapes=[pltpu.SemaphoreType.DMA((3,))],
         compiler_params=PARAMS,
         cost_estimate=cost(0, 18 << 20),
         name="hold",
-    )(side, parts, left, right)
+    )(side, scale, parts, left, right)
 
 
 def turn(shares, momentum, left):
@@ -196,21 +214,17 @@
     )(arrived, second, right, right_turned)
 
 
-def back(scale, arrived, left):
+def back(scale, arrived, left, moment_new, second_new):
     return pl.pallas_call(
         back_kernel,
-        out_shape=strips(),
-        in_specs=[VMEM, VMEM, VMEM],
-        out_specs=ANY,
+        out_shape=(strips(), strips(), strips()),
+        in_specs=[VMEM] * 5,
+        out_specs=(ANY, ANY, ANY),
         scratch_shapes=FRESH,
         compiler_params=PARAMS,
         cost_estimate=cost(32, 5 << 20),
         name="back",
-    )(scale, arrived, left)
-
-
-def spread(scale):
-    return jnp.broadcast_to(scale[:, None, None], (2, 16, 128))
+    )(scale, arrived, left, moment_new, second_new)
 
 
 def trade(message):
@@ -222,13 +236,14 @@
     side = lax.axis_index("xl").reshape(1)
     away = take_away(side, parts)
     came = lax.ppermute(away, "xl", [(0, 1), (1, 0)])
-    kept, left, right, right_turned, left_turned = hold(side, parts, left_basis, right_basis)
+    kept, left, right, right_turned, left_turned, scale_rows = hold(
+        side, lr_scale, parts, left_basis, right_basis
+    )
     pair = (kept.astype(F32) + came.astype(F32)).astype(BF16)
     shares = lax.all_to_all(pair, "z", split_axis=0, concat_axis=0, tiled=True)
-    momentum_out, message = turn(shares, momentum, left)
-    second_out, message = step(trade(message), second_moment, right, right_turned)
-    update = back(spread(lr_scale), trade(message), left_turned)
-    return (update, momentum_out, second_out)
+    moment_new, message = turn(shares, momentum, left)
+    second_new, message = step(trade(message), second_moment, right, right_turned)
+    return back(scale_rows, trade(message), left_turned, moment_new, second_new)
 
 
 def solution(mesh):

time: 101 us -> 100 us (0.990)
  blocking collectives: 81.9 us -> 79.5 us
  local copies, waits for them, and re-layouts: 5.67 us -> 7.48 us
    all_to_all x1, blocking collectives: 35.1 us -> 32.6 us  [local(): shares = lax.all_to_all(pair, 'z', split_axis=0, concat_axis=0, tiled=True)]
    unnamed x12 -> x14, local copies, waits for them, and re-layouts: 5.6 us -> 7.48 us
  transfers between devices with their start and end apart: 1 -> 1, of which waited for: 0 -> 0; matrix products, arithmetic and copies ran while one was open for 0% -> 0% of each run, Pallas kernels for 3% -> 4%
where the time goes in v5:
time: 100 us; the launch traced here: 99.8 us
  blocking collectives  79.5 us (80%)
  Pallas kernels  7.91 us (8%)
  local copies, waits for them, and re-layouts  7.48 us (7%)
  starting transfers between devices  3.95 us (4%)
    all_to_all x2, blocking collectives, trade(): return lax.all_to_all(message, MP, split_axis=0, concat_axis=0, tiled=True)  46.9 us
    all_to_all x1, blocking collectives, local(): shares = lax.all_to_all(pair, 'z', split_axis=0, concat_axis=0, tiled=True)  32.6 us
    unnamed x14, local copies, waits for them, and re-layouts  7.48 us
    ppermute x1, starting transfers between devices, local(): came = lax.ppermute(away, 'xl', [(0, 1), (1, 0)])  3.95 us
    pallas_call x1, Pallas kernels, hold(): pl.pallas_call(hold_kernel, out_shape=(half(), basis, basis, basis, basis...  3.57 us
  transfers between devices with their start and end apart: 1, of which 0 were waited for; matrix products, arithmetic and copies ran while one was open for 0% of the time, Pallas kernels for 4%

profile of v5, /device:TPU:1, one launch (start us, length us, event | category | flops | bytes accessed | tf_op | source)
XLA Modules:
  0.0 99.8 jit_solution(593262674001532007)
XLA Ops:
  0.6 0.0 copy-start.2
  0.6 1.2 %copy-done.2 = bf16[1,32,16,1024]{3,2,1,0:T(8,128)(2,1)S(1)} copy-done((bf16[1,32,16,1024]{3,2,1,0:T(8,128)(2,1)S(1)}, bf16[1,32,16,1024]{3,2,1,0:T(8,128)(2,1)}, u32[]{:S(2)}) %copy-start.2) | copy-done | bytes 1048600
  1.9 3.9 %collective-permute-start = (bf16[8,2,16,1024]{3,2,1,0:T(8,128)(2,1)S(1)}, bf16[8,2,16,1024]{3,2,1,0:T(8,128)(2,1)S(1)}, u32[]{:S(2)}, u32[]{:S(2)}) collective-permute-start(bf16[8,2,16,1024]{3,2,1,0:T(8,128)(2,1)S(1)} %take_away.1), channel_id=1, source_target_pairs={{0,64},{64,0},{1,65},{65,1},{2,66},{66,2},{3,67},{67,3},{4,68},{68... | collective-permute-start | bytes 1572872 | tf_op jit(solution)/shard_map/ppermute | solution.py:238
  5.9 0.0 copy-start
  5.9 2.2 %copy-done = bf16[2,1024,1024]{2,1,0:T(8,128)(2,1)S(1)} copy-done((bf16[2,1024,1024]{2,1,0:T(8,128)(2,1)S(1)}, bf16[2,1024,1024]{2,1,0:T(8,128)(2,1)}, u32[]{:S(2)}) %copy-start) | copy-done | bytes 4194328
  8.1 0.0 copy-start.1
  8.1 2.2 %copy-done.1 = bf16[2,1024,1024]{2,1,0:T(8,128)(2,1)S(1)} copy-done((bf16[2,1024,1024]{2,1,0:T(8,128)(2,1)S(1)}, bf16[2,1024,1024]{2,1,0:T(8,128)(2,1)}, u32[]{:S(2)}) %copy-start.1) | copy-done | bytes 4194328
  10.3 0.0 copy-start.3
  10.3 1.2 %copy-done.3 = bf16[1,32,16,1024]{3,2,1,0:T(8,128)(2,1)S(1)} copy-done((bf16[1,32,16,1024]{3,2,1,0:T(8,128)(2,1)S(1)}, bf16[1,32,16,1024]{3,2,1,0:T(8,128)(2,1)}, u32[]{:S(2)}) %copy-start.3) | copy-done | bytes 1048600
  11.5 0.0 copy-start.6
  11.5 0.7 copy-done.6
  12.1 0.0 copy-start.5
  12.1 3.6 %hold.1 = (bf16[8,2,16,1024]{3,2,1,0:T(8,128)(2,1)S(1)}, bf16[2,1024,1024]{2,1,0:T(8,128)(2,1)S(1)}, bf16[2,1024,1024]{2,1,0:T(8,128)(2,1)S(1)}, bf16[2,1024,102...) custom-call(s32[1]{0:T(128)} %bitcast.side, f32[2]{0:T(128)S(1)} %copy-done.6, ...), custom_call_target="tpu_custom_call" | custom-call | bytes 18874368 | tf_op jit(solution)/shard_map/hold/pallas_call | solution.py:181
  15.7 0.0 copy-start.4
  15.7 0.0 collective-permute-done
  15.7 0.2 add_convert_fusion
  15.9 32.6 %all_to_all.27.shares = bf16[8,2,16,1024]{3,2,1,0:T(8,128)(2,1)S(1)} all-to-all(bf16[8,2,16,1024]{3,2,1,0:T(8,128)(2,1)S(1)} %add_convert_fusion), channel_id=1, replica_groups=mesh['z'=8,'xl'=2,'y'=8,'xh'=4,'c'=2] {'z'}, dimensions={0} | all-to-all | bytes 1048576 | tf_op jit(solution)/shard_map/all_to_all | solution.py:243
  48.6 0.0 copy-done.5
  48.6 1.1 %turn.1 = (f32[2,16,1024]{2,1,0:T(8,128)S(1)}, bf16[512,128]{1,0:T(8,128)(2,1)S(1)}) custom-call(bf16[8,2,16,1024]{3,2,1,0:T(8,128)(2,1)S(1)} %all_to_all.27.shares, f32[2,16,1024]{2,1,0:T(8,128)S(1)} %copy-done.5, bf16[2,1024,1024]{2,1,0:T(8,128)(2,1)S(1)} %get-tuple-element.15.left), custom_call_target="tpu_custom_call" | custom-call | flops 134217728 | bytes 5242880 | tf_op jit(solution)/shard_map/turn/pallas_call | solution.py:194
  49.7 29.7 %all_to_all.28 = bf16[64,8,128]{2,1,0:T(8,128)(2,1)S(1)} all-to-all(bf16[64,8,128]{2,1,0:T(8,128)(2,1)S(1)} %bitcast.11), channel_id=1, replica_groups=mesh['z'=8,'xl'=2,'y'=8,'xh'=4,'c'=2] {'y','xh','c'}, dimensions={0} | all-to-all | bytes 262144 | tf_op jit(solution)/shard_map/all_to_all | solution.py:231
  79.3 0.0 copy-done.4
  79.3 1.8 %step.1 = (f32[2,16,1024]{2,1,0:T(8,128)S(1)}, bf16[512,128]{1,0:T(8,128)(2,1)S(1)}) custom-call(bf16[512,128]{1,0:T(8,128)(2,1)S(1)} %bitcast.8, f32[2,16,1024]{2,1,0:T(8,128)S(1)} %copy-done.4, bf16[2,1024,1024]{2,1,0:T(8,128)(2,1)S(1)} %get-tuple-element.17.right, bf16[2,1024,1024]{2,1,0:T(8,128)(2,1)S(1)} %get-tuple-element.18.right_turned), custom_call_target="tpu_custom_call" | custom-call | flops 201326592 | bytes 5242880 | tf_op jit(solution)/shard_map/step/pallas_call | solution.py:206
  81.1 17.2 %all_to_all.29 = bf16[64,8,128]{2,1,0:T(8,128)(2,1)S(1)} all-to-all(bf16[64,8,128]{2,1,0:T(8,128)(2,1)S(1)} %bitcast.10), channel_id=1, replica_groups=mesh['z'=8,'xl'=2,'y'=8,'xh'=4,'c'=2] {'y','xh','c'}, dimensions={0} | all-to-all | bytes 262144 | tf_op jit(solution)/shard_map/all_to_all | solution.py:231
  98.3 1.4 %back.1 = (f32[2,16,1024]{2,1,0:T(8,128)}, f32[2,16,1024]{2,1,0:T(8,128)}, f32[2,16,1024]{2,1,0:T(8,128)}) custom-call(f32[2,16,128]{2,1,0:T(8,128)S(1)} %get-tuple-element.13.scale, bf16[512,128]{1,0:T(8,128)(2,1)S(1)} %bitcast.9, bf16[2,1024,1024]{2,1,0:T(8,128)(2,1)S(1)} %get-tuple-element.20.left, f32[2,16,1024]{2,1,0:T(8,128)S(1)} %get-tuple-element.21.moment_new, ...), custom_call_target="tpu_custom_call" | custom-call | flops 67108864 | bytes 5242880 | tf_op jit(solution)/shard_map/back/pallas_call | solution.py:218
  (1 shorter events, 0.0 us)
Async XLA Ops:
  0.6 1.2 %copy-start.2 = (bf16[1,32,16,1024]{3,2,1,0:T(8,128)(2,1)S(1)}, bf16[1,32,16,1024]{3,2,1,0:T(8,128)(2,1)}, u32[]{:S(2)}) copy-start(bf16[1,32,16,1024]{3,2,1,0:T(8,128)(2,1)} %param.6) | copy-start | bytes 3145732
  1.9 13.8 %collective-permute-start = (bf16[8,2,16,1024]{3,2,1,0:T(8,128)(2,1)S(1)}, bf16[8,2,16,1024]{3,2,1,0:T(8,128)(2,1)S(1)}, u32[]{:S(2)}, u32[]{:S(2)}) collective-permute-start(bf16[8,2,16,1024]{3,2,1,0:T(8,128)(2,1)S(1)} %take_away.1), channel_id=1, source_target_pairs={{0,64},{64,0},{1,65},{65,1},{2,66},{66,2},{3,67},{67,3},{4,68},{68... | collective-permute-start | bytes 1572872 | tf_op jit(solution)/shard_map/ppermute | solution.py:238
  5.9 2.2 %copy-start = (bf16[2,1024,1024]{2,1,0:T(8,128)(2,1)S(1)}, bf16[2,1024,1024]{2,1,0:T(8,128)(2,1)}, u32[]{:S(2)}) copy-start(bf16[2,1024,1024]{2,1,0:T(8,128)(2,1)} %left.1) | copy-start | bytes 12582916
  8.1 2.2 %copy-start.1 = (bf16[2,1024,1024]{2,1,0:T(8,128)(2,1)S(1)}, bf16[2,1024,1024]{2,1,0:T(8,128)(2,1)}, u32[]{:S(2)}) copy-start(bf16[2,1024,1024]{2,1,0:T(8,128)(2,1)} %right.1) | copy-start | bytes 12582916
  10.3 1.2 %copy-start.3 = (bf16[1,32,16,1024]{3,2,1,0:T(8,128)(2,1)S(1)}, bf16[1,32,16,1024]{3,2,1,0:T(8,128)(2,1)}, u32[]{:S(2)}) copy-start(bf16[1,32,16,1024]{3,2,1,0:T(8,128)(2,1)} %param.6) | copy-start | bytes 3145732
  11.5 0.7 copy-start.6
  12.1 36.5 %copy-start.5 = (f32[2,16,1024]{2,1,0:T(8,128)S(1)}, f32[2,16,1024]{2,1,0:T(8,128)}, u32[]{:S(2)}) copy-start(f32[2,16,1024]{2,1,0:T(8,128)} %moment.1) | copy-start | bytes 393220
  15.7 63.6 %copy-start.4 = (f32[2,16,1024]{2,1,0:T(8,128)S(1)}, f32[2,16,1024]{2,1,0:T(8,128)}, u32[]{:S(2)}) copy-start(f32[2,16,1024]{2,1,0:T(8,128)} %second.1) | copy-start | bytes 393220

commit v6 on v5

--- a/solution.py
+++ b/solution.py
@@ -107,35 +107,26 @@
         write.wait()
 
 
-def away_kernel(side, parts, away, sem):
-    copy = pltpu.make_async_copy(parts.at[:, 1 - side[0]], away, sem)
-    copy.start()
-    copy.wait()
-
-
-def hold_kernel(
-    side,
-    scale,
-    parts,
-    left,
-    right,
-    kept,
-    left_held,
-    right_held,
-    right_turned,
-    left_turned,
-    scale_rows,
-    sems,
-):
+def split_kernel(side, parts, first, last, kept, sems):
     copies = [
-        pltpu.make_async_copy(parts.at[:, side[0]], kept, sems.at[0]),
-        pltpu.make_async_copy(left, left_held, sems.at[1]),
-        pltpu.make_async_copy(right, right_held, sems.at[2]),
+        pltpu.make_async_copy(parts.at[pl.ds(0, 4), 1 - side[0]], first, sems.at[0]),
+        pltpu.make_async_copy(parts.at[pl.ds(4, 4), 1 - side[0]], last, sems.at[1]),
+        pltpu.make_async_copy(parts.at[:, side[0]], kept, sems.at[2]),
     ]
     for copy in copies:
         copy.start()
-    for b in range(2):
-        scale_rows[b] = jnp.full((16, 128), scale[b], F32)
+    for copy in copies:
+        copy.wait()
+
+
+def hold_kernel(left, right, left_held, right_held, right_turned, left_turned, sems):
+    copies = [
+        pltpu.make_async_copy(left, left_held, sems.at[0]),
+        pltpu.make_async_copy(right, right_held, sems.at[1]),
+    ]
+    for copy in copies:
+        copy.start()
+    for b in range(2):
         left_turned[b] = left[b].T
         right_turned[b] = right[b].T
     for copy in copies:
@@ -155,39 +146,36 @@
 
 
 FRESH = [pltpu.VMEM((2, 16, 1024), F32), pltpu.SemaphoreType.DMA((4,))]
-HBM = pl.BlockSpec(memory_space=pltpu.HBM)
 ANY = pl.BlockSpec(memory_space=pl.ANY)
 
 
-def half():
-    return jax.ShapeDtypeStruct((8, 2, 16, 1024), BF16)
-
-
-def take_away(side, parts):
-    return pl.pallas_call(
-        away_kernel,
-        out_shape=half(),
-        in_specs=[SMEM, HBM],
-        out_specs=ANY,
-        scratch_shapes=[pltpu.SemaphoreType.DMA],
-        compiler_params=PARAMS,
-        cost_estimate=cost(0, 1 << 20),
-        name="take_away",
+def split(side, parts):
+    quarter = jax.ShapeDtypeStruct((4, 2, 16, 1024), BF16)
+    half = jax.ShapeDtypeStruct((8, 2, 16, 1024), BF16)
+    return pl.pallas_call(
+        split_kernel,
+        out_shape=(quarter, quarter, half),
+        in_specs=[SMEM, ANY],
+        out_specs=(ANY, ANY, ANY),
+        scratch_shapes=[pltpu.SemaphoreType.DMA((3,))],
+        compiler_params=PARAMS,
+        cost_estimate=cost(0, 2 << 20),
+        name="split",
     )(side, parts)
 
 
-def hold(side, scale, parts, left, right):
+def hold(left, right):
     basis = jax.ShapeDtypeStruct((2, 1024, 1024), BF16)
     return pl.pallas_call(
         hold_kernel,
-        out_shape=(half(), basis, basis, basis, basis, jax.ShapeDtypeStruct((2, 16, 128), F32)),
-        in_specs=[SMEM, SMEM, HBM, VMEM, VMEM],
-        out_specs=(ANY, ANY, ANY, VMEM, VMEM, VMEM),
-        scratch_shapes=[pltpu.SemaphoreType.DMA((3,))],
-        compiler_params=PARAMS,
-        cost_estimate=cost(0, 18 << 20),
+        out_shape=(basis, basis, basis, basis),
+        in_specs=[VMEM, VMEM],
+        out_specs=(ANY, ANY, VMEM, VMEM),
+        scratch_shapes=[pltpu.SemaphoreType.DMA((2,))],
+        compiler_params=PARAMS,
+        cost_estimate=cost(0, 24 << 20),
         name="hold",
-    )(side, scale, parts, left, right)
+    )(left, right)
 
 
 def turn(shares, momentum, left):
@@ -234,13 +222,12 @@
 def local(grad_parts, momentum, second_moment, left_basis, right_basis, lr_scale):
     parts = grad_parts[0].reshape(8, 2, 2, 16, 1024)
     side = lax.axis_index("xl").reshape(1)
-    away = take_away(side, parts)
-    came = lax.ppermute(away, "xl", [(0, 1), (1, 0)])
-    kept, left, right, right_turned, left_turned, scale_rows = hold(
-        side, lr_scale, parts, left_basis, right_basis
-    )
-    pair = (kept.astype(F32) + came.astype(F32)).astype(BF16)
+    *away, kept = split(side, parts)
+    came = [lax.ppermute(piece, "xl", [(0, 1), (1, 0)]) for piece in away]
+    left, right, right_turned, left_turned = hold(left_basis, right_basis)
+    pair = (kept.astype(F32) + jnp.concatenate(came).astype(F32)).astype(BF16)
     shares = lax.all_to_all(pair, "z", split_axis=0, concat_axis=0, tiled=True)
+    scale_rows = jnp.broadcast_to(lr_scale[:, None, None], (2, 16, 128))
     moment_new, message = turn(shares, momentum, left)
     second_new, message = step(trade(message), second_moment, right, right_turned)
     return back(scale_rows, trade(message), left_turned, moment_new, second_new)

time: 100 us -> 106 us (1.060)
  blocking collectives: 79.5 us -> 45.8 us
  starting transfers between devices: 3.95 us -> 26.5 us
  local copies, waits for them, and re-layouts: 7.48 us -> 17.9 us
  waiting for transfers between devices: 0.01 us -> 6.15 us
    all_to_all x1 -> x0, blocking collectives: 32.6 us -> none  [local(): shares = lax.all_to_all(pair, 'z', split_axis=0, concat_axis=0, tiled=True)]
    all_to_all x0 -> x1, starting transfers between devices: none -> 20.6 us  [local(): shares = lax.all_to_all(pair, 'z', split_axis=0, concat_axis=0, tiled=True)]
    unnamed x14 -> x28, local copies, waits for them, and re-layouts: 7.48 us -> 17.8 us
    ppermute x1 -> x2, waiting for transfers between devices: 0.01 us -> 5.45 us  [local(): came = [lax.ppermute(piece, 'xl', [(0, 1), (1, 0)]) for piece in away]]
    ppermute x1 -> x2, starting transfers between devices: 3.95 us -> 5.87 us  [local(): came = [lax.ppermute(piece, 'xl', [(0, 1), (1, 0)]) for piece in away]]
  transfers between devices with their start and end apart: 1 -> 3, of which waited for: 0 -> 3; matrix products, arithmetic and copies ran while one was open for 0% -> 0% of each run, Pallas kernels for 4% -> 3%
where the time goes in v6:
time: 106 us; the launch traced here: 105 us
  blocking collectives  45.8 us (43%)
  starting transfers between devices  26.5 us (25%)
  local copies, waits for them, and re-layouts  17.9 us (17%)
  Pallas kernels  7.35 us (7%)
  waiting for transfers between devices  6.15 us (6%)
    all_to_all x2, blocking collectives, trade(): return lax.all_to_all(message, MP, split_axis=0, concat_axis=0, tiled=True)  45.8 us
    all_to_all x1, starting transfers between devices, local(): shares = lax.all_to_all(pair, 'z', split_axis=0, concat_axis=0, tiled=True)  20.6 us
    unnamed x28, local copies, waits for them, and re-layouts  17.8 us
    ppermute x2, starting transfers between devices, local(): came = [lax.ppermute(piece, 'xl', [(0, 1), (1, 0)]) for piece in away]  5.87 us
    ppermute x2, waiting for transfers between devices, local(): came = [lax.ppermute(piece, 'xl', [(0, 1), (1, 0)]) for piece in away]  5.45 us
    pallas_call x1, Pallas kernels, hold(): pl.pallas_call(hold_kernel, out_shape=(basis, basis, basis, basis), in_sp...  2.98 us
  transfers between devices with their start and end apart: 3, of which 3 were waited for; matrix products, arithmetic and copies ran while one was open for 0% of the time, Pallas kernels for 3%

profile of v6, /device:TPU:1, one launch (start us, length us, event | category | flops | bytes accessed | tf_op | source)
XLA Modules:
  0.0 105.4 jit_solution(9865526374320310560)
XLA Ops:
  0.6 0.0 copy-start.10
  0.6 1.2 %copy-done.10 = bf16[1,32,16,1024]{3,2,1,0:T(8,128)(2,1)S(1)} copy-done((bf16[1,32,16,1024]{3,2,1,0:T(8,128)(2,1)S(1)}, bf16[1,32,16,1024]{3,2,1,0:T(8,128)(2,1)}, u32[]{:S(2)}) %copy-start.10) | copy-done | bytes 1048600
  1.9 0.1 split.1
  2.0 3.9 %collective-permute-start = (bf16[4,2,16,1024]{3,2,1,0:T(8,128)(2,1)S(1)}, bf16[4,2,16,1024]{3,2,1,0:T(8,128)(2,1)S(1)}, u32[]{:S(2)}, u32[]{:S(2)}) collective-permute-start(bf16[4,2,16,1024]{3,2,1,0:T(8,128)(2,1)S(1)} %get-tuple-element.15), channel_id=1, source_target_pairs={{0,64},{64,0},{1,65},{65,1},{2,66},{66,2},{3,67},{67,3},{4,68},{68... | collective-permute-start | bytes 786440 | tf_op jit(solution)/shard_map/ppermute | solution.py:226
  5.9 1.9 %collective-permute-start.1 = (bf16[4,2,16,1024]{3,2,1,0:T(8,128)(2,1)S(1)}, bf16[4,2,16,1024]{3,2,1,0:T(8,128)(2,1)S(1)}, u32[]{:S(2)}, u32[]{:S(2)}) collective-permute-start(bf16[4,2,16,1024]{3,2,1,0:T(8,128)(2,1)S(1)} %get-tuple-element.16), channel_id=1, source_target_pairs={{0,64},{64,0},{1,65},{65,1},{2,66},{66,2},{3,67},{67,3},{4,68},{68... | collective-permute-start | bytes 786440 | tf_op jit(solution)/shard_map/ppermute | solution.py:226
  7.9 2.0 %collective-permute-done = bf16[4,2,16,1024]{3,2,1,0:T(8,128)(2,1)S(1)} collective-permute-done((bf16[4,2,16,1024]{3,2,1,0:T(8,128)(2,1)S(1)}, bf16[4,2,16,1024]{3,2,1,0:T(8,128)(2,1)S(1)}, u32[]{:S(2)}, u32[]{:S(2)}) %collective-permute-start) | collective-permute-done | bytes 262176 | tf_op jit(solution)/shard_map/ppermute | solution.py:226
  9.8 3.5 %collective-permute-done.1 = bf16[4,2,16,1024]{3,2,1,0:T(8,128)(2,1)S(1)} collective-permute-done((bf16[4,2,16,1024]{3,2,1,0:T(8,128)(2,1)S(1)}, bf16[4,2,16,1024]{3,2,1,0:T(8,128)(2,1)S(1)}, u32[]{:S(2)}, u32[]{:S(2)}) %collective-permute-start.1) | collective-permute-done | bytes 262176 | tf_op jit(solution)/shard_map/ppermute | solution.py:226
  13.3 1.0 add_convert_fusion
  14.3 20.6 %all-to-all-start = ((bf16[8,2,16,1024]{3,2,1,0:T(8,128)(2,1)}), bf16[8,2,16,1024]{3,2,1,0:T(8,128)(2,1)S(1)}, u32[]{:S(2)}, u32[]{:S(2)}) async-start(bf16[8,2,16,1024]{3,2,1,0:T(8,128)(2,1)} %add_convert_fusion), calls=%async_computation | async-start | bytes 1048576 | tf_op jit(solution)/shard_map/all_to_all | solution.py:229
  34.9 0.0 copy-start.2
  34.9 2.2 %copy-done.2 = bf16[2,1024,1024]{2,1,0:T(8,128)(2,1)S(1)} copy-done((bf16[2,1024,1024]{2,1,0:T(8,128)(2,1)S(1)}, bf16[2,1024,1024]{2,1,0:T(8,128)(2,1)}, u32[]{:S(2)}) %copy-start.2) | copy-done | bytes 4194328
  37.1 0.0 copy-start.3
  37.1 2.2 %copy-done.3 = bf16[2,1024,1024]{2,1,0:T(8,128)(2,1)S(1)} copy-done((bf16[2,1024,1024]{2,1,0:T(8,128)(2,1)S(1)}, bf16[2,1024,1024]{2,1,0:T(8,128)(2,1)}, u32[]{:S(2)}) %copy-start.3) | copy-done | bytes 4194328
  39.3 0.0 copy-start.12
  39.3 0.0 copy-start.11
  39.3 3.0 %hold.1 = (bf16[2,1024,1024]{2,1,0:T(8,128)(2,1)S(1)}, bf16[2,1024,1024]{2,1,0:T(8,128)(2,1)S(1)}, bf16[2,1024,1024]{2,1,0:T(8,128)(2,1)S(1)}, bf16[2,1024,1024]{2,1,0:T(8,128)(2,1)S(1)}) custom-call(bf16[2,1024,1024]{2,1,0:T(8,128)(2,1)S(1)} %copy-done.2, bf16[2,1024,1024]{2,1,0:T(8,128)(2,1)S(1)} %copy-done.3), custom_call_target="tpu_custom_call" | custom-call | bytes 25165824 | tf_op jit(solution)/shard_map/hold/pallas_call | solution.py:169
  42.3 0.0 copy-start
  42.3 2.0 %copy-done = bf16[2,1024,1024]{2,1,0:T(8,128)(2,1)} copy-done((bf16[2,1024,1024]{2,1,0:T(8,128)(2,1)}, bf16[2,1024,1024]{2,1,0:T(8,128)(2,1)S(1)}, u32[]{:S(2)}) %copy-start) | copy-done | bytes 4194328
  44.3 0.0 copy-start.4
  44.3 1.9 %copy-done.4 = bf16[2,1024,1024]{2,1,0:T(8,128)(2,1)} copy-done((bf16[2,1024,1024]{2,1,0:T(8,128)(2,1)}, bf16[2,1024,1024]{2,1,0:T(8,128)(2,1)S(1)}, u32[]{:S(2)}) %copy-start.4) | copy-done | bytes 4194328
  46.2 0.0 copy-start.6
  46.2 2.0 %copy-done.6 = bf16[2,1024,1024]{2,1,0:T(8,128)(2,1)} copy-done((bf16[2,1024,1024]{2,1,0:T(8,128)(2,1)}, bf16[2,1024,1024]{2,1,0:T(8,128)(2,1)S(1)}, u32[]{:S(2)}) %copy-start.6) | copy-done | bytes 4194328
  48.2 0.0 copy-start.8
  48.2 1.9 %copy-done.8 = bf16[2,1024,1024]{2,1,0:T(8,128)(2,1)} copy-done((bf16[2,1024,1024]{2,1,0:T(8,128)(2,1)}, bf16[2,1024,1024]{2,1,0:T(8,128)(2,1)S(1)}, u32[]{:S(2)}) %copy-start.8) | copy-done | bytes 4194328
  50.1 0.7 all-to-all-done.shares
  50.8 0.0 copy-done.12
  50.8 0.0 copy-start.1
  50.8 2.2 %copy-done.1 = bf16[2,1024,1024]{2,1,0:T(8,128)(2,1)S(1)} copy-done((bf16[2,1024,1024]{2,1,0:T(8,128)(2,1)S(1)}, bf16[2,1024,1024]{2,1,0:T(8,128)(2,1)}, u32[]{:S(2)}) %copy-start.1) | copy-done | bytes 4194328
  53.0 0.0 copy-start.7
  53.0 1.1 %turn.1 = (f32[2,16,1024]{2,1,0:T(8,128)S(1)}, bf16[512,128]{1,0:T(8,128)(2,1)S(1)}) custom-call(bf16[8,2,16,1024]{3,2,1,0:T(8,128)(2,1)S(1)} %all-to-all-done.shares, f32[2,16,1024]{2,1,0:T(8,128)S(1)} %copy-done.12, bf16[2,1024,1024]{2,1,0:T(8,128)(2,1)S(1)} %copy-done.1), custom_call_target="tpu_custom_call" | custom-call | flops 134217728 | bytes 5242880 | tf_op jit(solution)/shard_map/turn/pallas_call | solution.py:182
  54.1 28.6 %all_to_all.27 = bf16[64,8,128]{2,1,0:T(8,128)(2,1)S(1)} all-to-all(bf16[64,8,128]{2,1,0:T(8,128)(2,1)S(1)} %bitcast.10), channel_id=1, replica_groups=mesh['z'=8,'xl'=2,'y'=8,'xh'=4,'c'=2] {'y','xh','c'}, dimensions={0} | all-to-all | bytes 262144 | tf_op jit(solution)/shard_map/all_to_all | solution.py:219
  82.7 0.0 copy-done.11
  82.7 0.0 copy-done.7
  82.7 0.0 copy-start.9
  82.7 2.2 %copy-done.9 = bf16[2,1024,1024]{2,1,0:T(8,128)(2,1)S(1)} copy-done((bf16[2,1024,1024]{2,1,0:T(8,128)(2,1)S(1)}, bf16[2,1024,1024]{2,1,0:T(8,128)(2,1)}, u32[]{:S(2)}) %copy-start.9) | copy-done | bytes 4194328
  84.9 0.0 copy-start.13
  84.9 0.0 copy-start.5
  84.9 1.8 %step.1 = (f32[2,16,1024]{2,1,0:T(8,128)S(1)}, bf16[512,128]{1,0:T(8,128)(2,1)S(1)}) custom-call(bf16[512,128]{1,0:T(8,128)(2,1)S(1)} %bitcast.7, f32[2,16,1024]{2,1,0:T(8,128)S(1)} %copy-done.11, bf16[2,1024,1024]{2,1,0:T(8,128)(2,1)S(1)} %copy-done.7, bf16[2,1024,1024]{2,1,0:T(8,128)(2,1)S(1)} %copy-done.9), custom_call_target="tpu_custom_call" | custom-call | flops 201326592 | bytes 5242880 | tf_op jit(solution)/shard_map/step/pallas_call | solution.py:194
  86.7 17.2 %all_to_all.28 = bf16[64,8,128]{2,1,0:T(8,128)(2,1)S(1)} all-to-all(bf16[64,8,128]{2,1,0:T(8,128)(2,1)S(1)} %bitcast.9), channel_id=1, replica_groups=mesh['z'=8,'xl'=2,'y'=8,'xh'=4,'c'=2] {'y','xh','c'}, dimensions={0} | all-to-all | bytes 262144 | tf_op jit(solution)/shard_map/all_to_all | solution.py:219
  103.9 0.0 copy-done.13
  103.9 0.1 broadcast_in_dim.2.scale
  104.0 0.0 copy-done.5
  104.0 1.4 %back.1 = (f32[2,16,1024]{2,1,0:T(8,128)}, f32[2,16,1024]{2,1,0:T(8,128)}, f32[2,16,1024]{2,1,0:T(8,128)}) custom-call(f32[2,16,128]{2,1,0:T(8,128)S(1)} %broadcast_in_dim.2.scale, bf16[512,128]{1,0:T(8,128)(2,1)S(1)} %bitcast.8, bf16[2,1024,1024]{2,1,0:T(8,128)(2,1)S(1)} %copy-done.5, f32[2,16,1024]{2,1,0:T(8,128)S(1)} %get-tuple-element.23.moment_new, ...), custom_call_target="tpu_custom_call" | custom-call | flops 67108864 | bytes 5242880 | tf_op jit(solution)/shard_map/back/pallas_call | solution.py:206
Async XLA Ops:
  0.6 1.2 %copy-start.10 = (bf16[1,32,16,1024]{3,2,1,0:T(8,128)(2,1)S(1)}, bf16[1,32,16,1024]{3,2,1,0:T(8,128)(2,1)}, u32[]{:S(2)}) copy-start(bf16[1,32,16,1024]{3,2,1,0:T(8,128)(2,1)} %param.6) | copy-start | bytes 3145732
  2.0 7.9 %collective-permute-start = (bf16[4,2,16,1024]{3,2,1,0:T(8,128)(2,1)S(1)}, bf16[4,2,16,1024]{3,2,1,0:T(8,128)(2,1)S(1)}, u32[]{:S(2)}, u32[]{:S(2)}) collective-permute-start(bf16[4,2,16,1024]{3,2,1,0:T(8,128)(2,1)S(1)} %get-tuple-element.15), channel_id=1, source_target_pairs={{0,64},{64,0},{1,65},{65,1},{2,66},{66,2},{3,67},{67,3},{4,68},{68... | collective-permute-start | bytes 786440 | tf_op jit(solution)/shard_map/ppermute | solution.py:226
  5.9 7.4 %collective-permute-start.1 = (bf16[4,2,16,1024]{3,2,1,0:T(8,128)(2,1)S(1)}, bf16[4,2,16,1024]{3,2,1,0:T(8,128)(2,1)S(1)}, u32[]{:S(2)}, u32[]{:S(2)}) collective-permute-start(bf16[4,2,16,1024]{3,2,1,0:T(8,128)(2,1)S(1)} %get-tuple-element.16), channel_id=1, source_target_pairs={{0,64},{64,0},{1,65},{65,1},{2,66},{66,2},{3,67},{67,3},{4,68},{68... | collective-permute-start | bytes 786440 | tf_op jit(solution)/shard_map/ppermute | solution.py:226
  14.3 36.5 %all-to-all-start = ((bf16[8,2,16,1024]{3,2,1,0:T(8,128)(2,1)}), bf16[8,2,16,1024]{3,2,1,0:T(8,128)(2,1)S(1)}, u32[]{:S(2)}, u32[]{:S(2)}) async-start(bf16[8,2,16,1024]{3,2,1,0:T(8,128)(2,1)} %add_convert_fusion), calls=%async_computation | async-start | bytes 1048576 | tf_op jit(solution)/shard_map/all_to_all | solution.py:229
  34.9 2.2 %copy-start.2 = (bf16[2,1024,1024]{2,1,0:T(8,128)(2,1)S(1)}, bf16[2,1024,1024]{2,1,0:T(8,128)(2,1)}, u32[]{:S(2)}) copy-start(bf16[2,1024,1024]{2,1,0:T(8,128)(2,1)} %left.1) | copy-start | bytes 12582916
  37.1 2.2 %copy-start.3 = (bf16[2,1024,1024]{2,1,0:T(8,128)(2,1)S(1)}, bf16[2,1024,1024]{2,1,0:T(8,128)(2,1)}, u32[]{:S(2)}) copy-start(bf16[2,1024,1024]{2,1,0:T(8,128)(2,1)} %right.1) | copy-start | bytes 12582916
  39.3 11.5 %copy-start.12 = (f32[2,16,1024]{2,1,0:T(8,128)S(1)}, f32[2,16,1024]{2,1,0:T(8,128)}, u32[]{:S(2)}) copy-start(f32[2,16,1024]{2,1,0:T(8,128)} %moment.1) | copy-start | bytes 393220
  39.3 43.4 %copy-start.11 = (f32[2,16,1024]{2,1,0:T(8,128)S(1)}, f32[2,16,1024]{2,1,0:T(8,128)}, u32[]{:S(2)}) copy-start(f32[2,16,1024]{2,1,0:T(8,128)} %second.1) | copy-start | bytes 393220
  42.3 2.0 %copy-start = (bf16[2,1024,1024]{2,1,0:T(8,128)(2,1)}, bf16[2,1024,1024]{2,1,0:T(8,128)(2,1)S(1)}, u32[]{:S(2)}) copy-start(bf16[2,1024,1024]{2,1,0:T(8,128)(2,1)S(1)} %get-tuple-element.17.left) | copy-start | bytes 12582916
  44.3 1.9 %copy-start.4 = (bf16[2,1024,1024]{2,1,0:T(8,128)(2,1)}, bf16[2,1024,1024]{2,1,0:T(8,128)(2,1)S(1)}, u32[]{:S(2)}) copy-start(bf16[2,1024,1024]{2,1,0:T(8,128)(2,1)S(1)} %get-tuple-element.22.left) | copy-start | bytes 12582916
  46.2 2.0 %copy-start.6 = (bf16[2,1024,1024]{2,1,0:T(8,128)(2,1)}, bf16[2,1024,1024]{2,1,0:T(8,128)(2,1)S(1)}, u32[]{:S(2)}) copy-start(bf16[2,1024,1024]{2,1,0:T(8,128)(2,1)S(1)} %get-tuple-element.19.right) | copy-start | bytes 12582916
  48.2 1.9 %copy-start.8 = (bf16[2,1024,1024]{2,1,0:T(8,128)(2,1)}, bf16[2,1024,1024]{2,1,0:T(8,128)(2,1)S(1)}, u32[]{:S(2)}) copy-start(bf16[2,1024,1024]{2,1,0:T(8,128)(2,1)S(1)} %get-tuple-element.20.right_turned) | copy-start | bytes 12582916
  50.8 2.2 %copy-start.1 = (bf16[2,1024,1024]{2,1,0:T(8,128)(2,1)S(1)}, bf16[2,1024,1024]{2,1,0:T(8,128)(2,1)}, u32[]{:S(2)}) copy-start(bf16[2,1024,1024]{2,1,0:T(8,128)(2,1)} %copy-done) | copy-start | bytes 12582916
  53.0 29.7 %copy-start.7 = (bf16[2,1024,1024]{2,1,0:T(8,128)(2,1)S(1)}, bf16[2,1024,1024]{2,1,0:T(8,128)(2,1)}, u32[]{:S(2)}) copy-start(bf16[2,1024,1024]{2,1,0:T(8,128)(2,1)} %copy-done.6) | copy-start | bytes 12582916
  82.7 2.2 %copy-start.9 = (bf16[2,1024,1024]{2,1,0:T(8,128)(2,1)S(1)}, bf16[2,1024,1024]{2,1,0:T(8,128)(2,1)}, u32[]{:S(2)}) copy-start(bf16[2,1024,1024]{2,1,0:T(8,128)(2,1)} %copy-done.8) | copy-start | bytes 12582916
  84.9 19.0 %copy-start.13 = (f32[2]{0:T(128)S(1)}, f32[2]{0:T(128)}, u32[]{:S(2)}) copy-start(f32[2]{0:T(128)} %param.11) | copy-start | bytes 28
  84.9 19.0 %copy-start.5 = (bf16[2,1024,1024]{2,1,0:T(8,128)(2,1)S(1)}, bf16[2,1024,1024]{2,1,0:T(8,128)(2,1)}, u32[]{:S(2)}) copy-start(bf16[2,1024,1024]{2,1,0:T(8,128)(2,1)} %copy-done.4) | copy-start | bytes 12582916

commit v7 on v6

--- a/solution.py
+++ b/solution.py
@@ -12,7 +12,9 @@
 bias_two = 1.0 - 0.95**10
 
 MP = ("y", "xh", "c")
-DP = ("z", "xl")
+DP = ("zh", "zl", "xl")
+NEAR = ("zl", "xl", "c")
+GROUP = DP + ("c",)
 F32 = jnp.float32
 BF16 = jnp.bfloat16
 VMEM = pl.BlockSpec(memory_space=pltpu.VMEM)
@@ -107,16 +109,23 @@
         write.wait()
 
 
-def split_kernel(side, parts, first, last, kept, sems):
-    copies = [
-        pltpu.make_async_copy(parts.at[pl.ds(0, 4), 1 - side[0]], first, sems.at[0]),
-        pltpu.make_async_copy(parts.at[pl.ds(4, 4), 1 - side[0]], last, sems.at[1]),
-        pltpu.make_async_copy(parts.at[:, side[0]], kept, sems.at[2]),
-    ]
-    for copy in copies:
-        copy.start()
-    for copy in copies:
-        copy.wait()
+def split_kernel(core, side, parts, away, kept, sems):
+    for index in range(2):
+
+        @pl.when(core[0] == index)
+        def _():
+            if index == 0:
+                sources = parts.at[:, :, 1 - side[0]], parts.at[:, :, side[0]]
+            else:
+                sources = parts.at[:, 1 - side[0]], parts.at[:, side[0]]
+            copies = [
+                pltpu.make_async_copy(source, out, sems.at[h])
+                for h, (source, out) in enumerate(zip(sources, (away, kept)))
+            ]
+            for copy in copies:
+                copy.start()
+            for copy in copies:
+                copy.wait()
 
 
 def hold_kernel(left, right, left_held, right_held, right_turned, left_turned, sems):
@@ -149,19 +158,18 @@
 ANY = pl.BlockSpec(memory_space=pl.ANY)
 
 
-def split(side, parts):
-    quarter = jax.ShapeDtypeStruct((4, 2, 16, 1024), BF16)
-    half = jax.ShapeDtypeStruct((8, 2, 16, 1024), BF16)
+def split(core, side, parts):
+    half = jax.ShapeDtypeStruct((4, 2, 2, 16, 1024), BF16)
     return pl.pallas_call(
         split_kernel,
-        out_shape=(quarter, quarter, half),
-        in_specs=[SMEM, ANY],
-        out_specs=(ANY, ANY, ANY),
-        scratch_shapes=[pltpu.SemaphoreType.DMA((3,))],
+        out_shape=(half, half),
+        in_specs=[SMEM, SMEM, ANY],
+        out_specs=(ANY, ANY),
+        scratch_shapes=[pltpu.SemaphoreType.DMA((2,))],
         compiler_params=PARAMS,
         cost_estimate=cost(0, 2 << 20),
         name="split",
-    )(side, parts)
+    )(core, side, parts)
 
 
 def hold(left, right):
@@ -219,22 +227,45 @@
     return lax.all_to_all(message, MP, split_axis=0, concat_axis=0, tiled=True)
 
 
+def near_pairs():
+    place = {(zl, xl, c): 4 * zl + 2 * xl + c for zl in (0, 1) for xl in (0, 1) for c in (0, 1)}
+    return [
+        (here, place[(zl, 1 - xl, c)] if c == 0 else place[(1 - zl, xl, c)])
+        for (zl, xl, c), here in place.items()
+    ]
+
+
+def sum_groups():
+    def place(zh, zl, xl, c):
+        return 8 * zh + 4 * zl + 2 * xl + c
+
+    along_z = [[place(zh, zl, xl, 0) for zh in range(4) for zl in (0, 1)] for xl in (0, 1)]
+    along_x = [[place(zh, zl, xl, 1) for zh in range(4) for xl in (0, 1)] for zl in (0, 1)]
+    return along_z + along_x
+
+
 def local(grad_parts, momentum, second_moment, left_basis, right_basis, lr_scale):
-    parts = grad_parts[0].reshape(8, 2, 2, 16, 1024)
-    side = lax.axis_index("xl").reshape(1)
-    *away, kept = split(side, parts)
-    came = [lax.ppermute(piece, "xl", [(0, 1), (1, 0)]) for piece in away]
-    left, right, right_turned, left_turned = hold(left_basis, right_basis)
-    pair = (kept.astype(F32) + jnp.concatenate(came).astype(F32)).astype(BF16)
-    shares = lax.all_to_all(pair, "z", split_axis=0, concat_axis=0, tiled=True)
+    parts = grad_parts[0].reshape(4, 2, 2, 2, 16, 1024)
+    core = lax.axis_index("c")
+    side = jnp.where(core == 0, lax.axis_index("xl"), lax.axis_index("zl")).reshape(1)
+    core = core.reshape(1)
+    away, kept = split(core, side, parts)
+    came = lax.ppermute(away, NEAR, near_pairs())
     scale_rows = jnp.broadcast_to(lr_scale[:, None, None], (2, 16, 128))
+    held = hold(left_basis, right_basis)
+    kept, scale_rows, held = lax.optimization_barrier((kept, scale_rows, held))
+    left, right, right_turned, left_turned = held
+    pair = (kept.astype(F32) + came.astype(F32)).astype(BF16).reshape(8, 2, 16, 1024)
+    shares = lax.all_to_all(
+        pair, GROUP, split_axis=0, concat_axis=0, axis_index_groups=sum_groups(), tiled=True
+    )
     moment_new, message = turn(shares, momentum, left)
     second_new, message = step(trade(message), second_moment, right, right_turned)
     return back(scale_rows, trade(message), left_turned, moment_new, second_new)
 
 
 def solution(mesh):
-    fine = Mesh(mesh.devices.reshape(8, 2, 8, 4, 2), DP + MP)
+    fine = Mesh(mesh.devices.reshape(4, 2, 2, 8, 4, 2), DP + MP)
     in_specs = (
         P(DP, None, MP, None),
         P(DP, MP, None),

time: 106 us -> 96 us (0.906)
  blocking collectives: 45.8 us -> 75.9 us
  starting transfers between devices: 26.5 us -> 5.74 us
  local copies, waits for them, and re-layouts: 17.9 us -> 5.67 us
  waiting for transfers between devices: 6.15 us -> 0.01 us
    all_to_all x0 -> x1, blocking collectives: none -> 28.5 us  [local(): lax.all_to_all(pair, GROUP, split_axis=0, concat_axis=0, axis_index_group...]
    all_to_all x1 -> x0, starting transfers between devices: 20.6 us -> none  [local(): shares = lax.all_to_all(pair, 'z', split_axis=0, concat_axis=0, tiled=True)]
    unnamed x28 -> x12, local copies, waits for them, and re-layouts: 17.8 us -> 5.6 us
    ppermute x2 -> x1, waiting for transfers between devices: 5.45 us -> 0.01 us  [local(): came = lax.ppermute(away, NEAR, near_pairs())]
    all_to_all x2, blocking collectives: 45.8 us -> 47.5 us  [trade(): return lax.all_to_all(message, MP, split_axis=0, concat_axis=0, tiled=True)]
    ppermute x2 -> x1, starting transfers between devices: 5.87 us -> 5.74 us  [local(): came = lax.ppermute(away, NEAR, near_pairs())]
  transfers between devices with their start and end apart: 3 -> 1, of which waited for: 3 -> 0; matrix products, arithmetic and copies ran while one was open for 0% -> 0% of each run, Pallas kernels for 3% -> 3%
where the time goes in v7:
time: 96 us; the launch traced here: 95.6 us
  blocking collectives  75.9 us (79%)
  Pallas kernels  7.34 us (8%)
  starting transfers between devices  5.74 us (6%)
  local copies, waits for them, and re-layouts  5.67 us (6%)
    all_to_all x2, blocking collectives, trade(): return lax.all_to_all(message, MP, split_axis=0, concat_axis=0, tiled=True)  47.5 us
    all_to_all x1, blocking collectives, local(): lax.all_to_all(pair, GROUP, split_axis=0, concat_axis=0, axis_index_group...  28.5 us
    ppermute x1, starting transfers between devices, local(): came = lax.ppermute(away, NEAR, near_pairs())  5.74 us
    unnamed x12, local copies, waits for them, and re-layouts  5.6 us
    pallas_call x1, Pallas kernels, hold(): pl.pallas_call(hold_kernel, out_shape=(basis, basis, basis, basis), in_sp...  2.98 us
  transfers between devices with their start and end apart: 1, of which 0 were waited for; matrix products, arithmetic and copies ran while one was open for 0% of the time, Pallas kernels for 3%

profile of v7, /device:TPU:1, one launch (start us, length us, event | category | flops | bytes accessed | tf_op | source)
XLA Modules:
  0.0 95.6 jit_solution(2350781885163057826)
XLA Ops:
  0.6 0.0 copy-start.2
  0.6 1.2 %copy-done.2 = bf16[1,32,16,1024]{3,2,1,0:T(8,128)(2,1)S(1)} copy-done((bf16[1,32,16,1024]{3,2,1,0:T(8,128)(2,1)S(1)}, bf16[1,32,16,1024]{3,2,1,0:T(8,128)(2,1)}, u32[]{:S(2)}) %copy-start.2) | copy-done | bytes 1048600
  1.9 0.1 split.1
  2.0 5.7 %collective-permute-start = (bf16[4,2,2,16,1024]{4,3,2,1,0:T(8,128)(2,1)S(1)}, bf16[4,2,2,16,1024]{4,3,2,1,0:T(8,128)(2,1)S(1)}, u32[]{:S(2)}, u32[]{:S(2)}) collective-permute-start(bf16[4,2,2,16,1024]{4,3,2,1,0:T(8,128)(2,1)S(1)} %get-tuple-element.26), channel_id=1, source_target_pairs={{0,64},{1,129},{64,0},{65,193},{128,192},{129,1},{192,128},{193,65... | collective-permute-start | bytes 1572872 | tf_op jit(solution)/shard_map/ppermute | solution.py:253
  7.7 0.0 copy-start
  7.7 2.2 %copy-done = bf16[2,1024,1024]{2,1,0:T(8,128)(2,1)S(1)} copy-done((bf16[2,1024,1024]{2,1,0:T(8,128)(2,1)S(1)}, bf16[2,1024,1024]{2,1,0:T(8,128)(2,1)}, u32[]{:S(2)}) %copy-start) | copy-done | bytes 4194328
  9.9 0.0 copy-start.1
  9.9 2.2 %copy-done.1 = bf16[2,1024,1024]{2,1,0:T(8,128)(2,1)S(1)} copy-done((bf16[2,1024,1024]{2,1,0:T(8,128)(2,1)S(1)}, bf16[2,1024,1024]{2,1,0:T(8,128)(2,1)}, u32[]{:S(2)}) %copy-start.1) | copy-done | bytes 4194328
  12.1 0.0 copy-start.5
  12.1 0.0 copy-start.4
  12.1 3.0 %hold.1 = (bf16[2,1024,1024]{2,1,0:T(8,128)(2,1)S(1)}, bf16[2,1024,1024]{2,1,0:T(8,128)(2,1)S(1)}, bf16[2,1024,1024]{2,1,0:T(8,128)(2,1)S(1)}, bf16[2,1024,1024]{2,1,0:T(8,128)(2,1)S(1)}) custom-call(bf16[2,1024,1024]{2,1,0:T(8,128)(2,1)S(1)} %copy-done, bf16[2,1024,1024]{2,1,0:T(8,128)(2,1)S(1)} %copy-done.1), custom_call_target="tpu_custom_call" | custom-call | bytes 25165824 | tf_op jit(solution)/shard_map/hold/pallas_call | solution.py:177
  15.1 0.0 copy-done.5
  15.1 0.0 copy-start.3
  15.1 0.1 broadcast_in_dim.2.scale
  15.2 0.0 collective-permute-done
  15.2 0.2 add_convert_fusion
  15.4 28.5 %all_to_all.27.shares = bf16[8,2,16,1024]{3,2,1,0:T(8,128)(2,1)S(1)} all-to-all(bf16[8,2,16,1024]{3,2,1,0:T(8,128)(2,1)S(1)} %bitcast.13), channel_id=1, replica_groups={{0,128,256,384,512,640,768,896},{64,192,320,448,576,704,832,960},{1,65,..., dimensions={0} | all-to-all | bytes 1048576 | tf_op jit(solution)/shard_map/all_to_all | solution.py:259
  43.9 0.0 copy-done.4
  43.9 1.1 %turn.1 = (f32[2,16,1024]{2,1,0:T(8,128)S(1)}, bf16[512,128]{1,0:T(8,128)(2,1)S(1)}) custom-call(bf16[8,2,16,1024]{3,2,1,0:T(8,128)(2,1)S(1)} %all_to_all.27.shares, f32[2,16,1024]{2,1,0:T(8,128)S(1)} %copy-done.4, bf16[2,1024,1024]{2,1,0:T(8,128)(2,1)S(1)} %get-tuple-element.27.left), custom_call_target="tpu_custom_call" | custom-call | flops 134217728 | bytes 5242880 | tf_op jit(solution)/shard_map/turn/pallas_call | solution.py:190
  45.0 30.3 %all_to_all.28 = bf16[64,8,128]{2,1,0:T(8,128)(2,1)S(1)} all-to-all(bf16[64,8,128]{2,1,0:T(8,128)(2,1)S(1)} %bitcast.12), channel_id=1, replica_groups=mesh['zh'=4,'zl'=2,'xl'=2,'y'=8,'xh'=4,'c'=2] {'y','xh','c'}, dimensions={0} | all-to-all | bytes 262144 | tf_op jit(solution)/shard_map/all_to_all | solution.py:227
  75.3 0.0 copy-done.3
  75.3 1.8 %step.1 = (f32[2,16,1024]{2,1,0:T(8,128)S(1)}, bf16[512,128]{1,0:T(8,128)(2,1)S(1)}) custom-call(bf16[512,128]{1,0:T(8,128)(2,1)S(1)} %bitcast.9, f32[2,16,1024]{2,1,0:T(8,128)S(1)} %copy-done.3, bf16[2,1024,1024]{2,1,0:T(8,128)(2,1)S(1)} %get-tuple-element.29.right, bf16[2,1024,1024]{2,1,0:T(8,128)(2,1)S(1)} %get-tuple-element.30.right_turned), custom_call_target="tpu_custom_call" | custom-call | flops 201326592 | bytes 5242880 | tf_op jit(solution)/shard_map/step/pallas_call | solution.py:202
  77.0 17.1 %all_to_all.29 = bf16[64,8,128]{2,1,0:T(8,128)(2,1)S(1)} all-to-all(bf16[64,8,128]{2,1,0:T(8,128)(2,1)S(1)} %bitcast.11), channel_id=1, replica_groups=mesh['zh'=4,'zl'=2,'xl'=2,'y'=8,'xh'=4,'c'=2] {'y','xh','c'}, dimensions={0} | all-to-all | bytes 262144 | tf_op jit(solution)/shard_map/all_to_all | solution.py:227
  94.2 1.4 %back.1 = (f32[2,16,1024]{2,1,0:T(8,128)}, f32[2,16,1024]{2,1,0:T(8,128)}, f32[2,16,1024]{2,1,0:T(8,128)}) custom-call(f32[2,16,128]{2,1,0:T(8,128)S(1)} %broadcast_in_dim.2.scale, bf16[512,128]{1,0:T(8,128)(2,1)S(1)} %bitcast.10, bf16[2,1024,1024]{2,1,0:T(8,128)(2,1)S(1)} %get-tuple-element.32.left, f32[2,16,1024]{2,1,0:T(8,128)S(1)} %get-tuple-element.33.moment_new, ...), custom_call_target="tpu_custom_call" | custom-call | flops 67108864 | bytes 5242880 | tf_op jit(solution)/shard_map/back/pallas_call | solution.py:214
Async XLA Ops:
  0.6 1.2 %copy-start.2 = (bf16[1,32,16,1024]{3,2,1,0:T(8,128)(2,1)S(1)}, bf16[1,32,16,1024]{3,2,1,0:T(8,128)(2,1)}, u32[]{:S(2)}) copy-start(bf16[1,32,16,1024]{3,2,1,0:T(8,128)(2,1)} %param.6) | copy-start | bytes 3145732
  2.0 13.2 %collective-permute-start = (bf16[4,2,2,16,1024]{4,3,2,1,0:T(8,128)(2,1)S(1)}, bf16[4,2,2,16,1024]{4,3,2,1,0:T(8,128)(2,1)S(1)}, u32[]{:S(2)}, u32[]{:S(2)}) collective-permute-start(bf16[4,2,2,16,1024]{4,3,2,1,0:T(8,128)(2,1)S(1)} %get-tuple-element.26), channel_id=1, source_target_pairs={{0,64},{1,129},{64,0},{65,193},{128,192},{129,1},{192,128},{193,65... | collective-permute-start | bytes 1572872 | tf_op jit(solution)/shard_map/ppermute | solution.py:253
  7.7 2.2 %copy-start = (bf16[2,1024,1024]{2,1,0:T(8,128)(2,1)S(1)}, bf16[2,1024,1024]{2,1,0:T(8,128)(2,1)}, u32[]{:S(2)}) copy-start(bf16[2,1024,1024]{2,1,0:T(8,128)(2,1)} %left.1) | copy-start | bytes 12582916
  9.9 2.2 %copy-start.1 = (bf16[2,1024,1024]{2,1,0:T(8,128)(2,1)S(1)}, bf16[2,1024,1024]{2,1,0:T(8,128)(2,1)}, u32[]{:S(2)}) copy-start(bf16[2,1024,1024]{2,1,0:T(8,128)(2,1)} %right.1) | copy-start | bytes 12582916
  12.1 3.0 %copy-start.5 = (f32[2]{0:T(128)S(1)}, f32[2]{0:T(128)}, u32[]{:S(2)}) copy-start(f32[2]{0:T(128)} %param.11) | copy-start | bytes 28
  12.1 31.8 %copy-start.4 = (f32[2,16,1024]{2,1,0:T(8,128)S(1)}, f32[2,16,1024]{2,1,0:T(8,128)}, u32[]{:S(2)}) copy-start(f32[2,16,1024]{2,1,0:T(8,128)} %moment.1) | copy-start | bytes 393220
  15.1 60.2 %copy-start.3 = (f32[2,16,1024]{2,1,0:T(8,128)S(1)}, f32[2,16,1024]{2,1,0:T(8,128)}, u32[]{:S(2)}) copy-start(f32[2,16,1024]{2,1,0:T(8,128)} %second.1) | copy-start | bytes 393220

commit v8 on v7

--- a/solution.py
+++ b/solution.py
@@ -114,7 +114,7 @@
 
         @pl.when(core[0] == index)
         def _():
-            if index == 0:
+            if index == 1:
                 sources = parts.at[:, :, 1 - side[0]], parts.at[:, :, side[0]]
             else:
                 sources = parts.at[:, 1 - side[0]], parts.at[:, side[0]]
@@ -230,7 +230,7 @@
 def near_pairs():
     place = {(zl, xl, c): 4 * zl + 2 * xl + c for zl in (0, 1) for xl in (0, 1) for c in (0, 1)}
     return [
-        (here, place[(zl, 1 - xl, c)] if c == 0 else place[(1 - zl, xl, c)])
+        (here, place[(zl, 1 - xl, c)] if c == 1 else place[(1 - zl, xl, c)])
         for (zl, xl, c), here in place.items()
     ]
 
@@ -239,15 +239,15 @@
     def place(zh, zl, xl, c):
         return 8 * zh + 4 * zl + 2 * xl + c
 
-    along_z = [[place(zh, zl, xl, 0) for zh in range(4) for zl in (0, 1)] for xl in (0, 1)]
-    along_x = [[place(zh, zl, xl, 1) for zh in range(4) for xl in (0, 1)] for zl in (0, 1)]
+    along_z = [[place(zh, zl, xl, 1) for zh in range(4) for zl in (0, 1)] for xl in (0, 1)]
+    along_x = [[place(zh, zl, xl, 0) for zh in range(4) for xl in (0, 1)] for zl in (0, 1)]
     return along_z + along_x
 
 
 def local(grad_parts, momentum, second_moment, left_basis, right_basis, lr_scale):
     parts = grad_parts[0].reshape(4, 2, 2, 2, 16, 1024)
     core = lax.axis_index("c")
-    side = jnp.where(core == 0, lax.axis_index("xl"), lax.axis_index("zl")).reshape(1)
+    side = jnp.where(core == 1, lax.axis_index("xl"), lax.axis_index("zl")).reshape(1)
     core = core.reshape(1)
     away, kept = split(core, side, parts)
     came = lax.ppermute(away, NEAR, near_pairs())

time: 96 us -> 95.6 us (level)
  starting transfers between devices: 5.74 us -> 3.95 us
  blocking collectives: 75.9 us -> 77.4 us
    all_to_all x1, blocking collectives: 28.5 us -> 34.3 us  [local(): lax.all_to_all(pair, GROUP, split_axis=0, concat_axis=0, axis_index_group...]
    all_to_all x2, blocking collectives: 47.5 us -> 43.1 us  [trade(): return lax.all_to_all(message, MP, split_axis=0, concat_axis=0, tiled=True)]
    ppermute x1, starting transfers between devices: 5.74 us -> 3.95 us  [local(): came = lax.ppermute(away, NEAR, near_pairs())]
where the time goes in v8:
time: 95.6 us; the launch traced here: 95.3 us
  blocking collectives  77.4 us (81%)
  Pallas kernels  7.34 us (8%)
  local copies, waits for them, and re-layouts  5.67 us (6%)
  starting transfers between devices  3.95 us (4%)
    all_to_all x2, blocking collectives, trade(): return lax.all_to_all(message, MP, split_axis=0, concat_axis=0, tiled=True)  43.1 us
    all_to_all x1, blocking collectives, local(): lax.all_to_all(pair, GROUP, split_axis=0, concat_axis=0, axis_index_group...  34.3 us
    unnamed x12, local copies, waits for them, and re-layouts  5.6 us
    ppermute x1, starting transfers between devices, local(): came = lax.ppermute(away, NEAR, near_pairs())  3.95 us
    pallas_call x1, Pallas kernels, hold(): pl.pallas_call(hold_kernel, out_shape=(basis, basis, basis, basis), in_sp...  2.98 us
  transfers between devices with their start and end apart: 1, of which 0 were waited for; matrix products, arithmetic and copies ran while one was open for 0% of the time, Pallas kernels for 3%

profile of v8, /device:TPU:1, one launch (start us, length us, event | category | flops | bytes accessed | tf_op | source)
XLA Modules:
  0.0 95.3 jit_solution(11320710866207567270)
XLA Ops:
  0.6 0.0 copy-start.2
  0.6 1.2 %copy-done.2 = bf16[1,32,16,1024]{3,2,1,0:T(8,128)(2,1)S(1)} copy-done((bf16[1,32,16,1024]{3,2,1,0:T(8,128)(2,1)S(1)}, bf16[1,32,16,1024]{3,2,1,0:T(8,128)(2,1)}, u32[]{:S(2)}) %copy-start.2) | copy-done | bytes 1048600
  1.9 0.1 split.1
  2.0 3.9 %collective-permute-start = (bf16[4,2,2,16,1024]{4,3,2,1,0:T(8,128)(2,1)S(1)}, bf16[4,2,2,16,1024]{4,3,2,1,0:T(8,128)(2,1)S(1)}, u32[]{:S(2)}, u32[]{:S(2)}) collective-permute-start(bf16[4,2,2,16,1024]{4,3,2,1,0:T(8,128)(2,1)S(1)} %get-tuple-element.26), channel_id=1, source_target_pairs={{0,128},{1,65},{64,192},{65,1},{128,0},{129,193},{192,64},{193,129... | collective-permute-start | bytes 1572872 | tf_op jit(solution)/shard_map/ppermute | solution.py:253
  5.9 0.0 copy-start
  5.9 2.2 %copy-done = bf16[2,1024,1024]{2,1,0:T(8,128)(2,1)S(1)} copy-done((bf16[2,1024,1024]{2,1,0:T(8,128)(2,1)S(1)}, bf16[2,1024,1024]{2,1,0:T(8,128)(2,1)}, u32[]{:S(2)}) %copy-start) | copy-done | bytes 4194328
  8.1 0.0 copy-start.1
  8.1 2.2 %copy-done.1 = bf16[2,1024,1024]{2,1,0:T(8,128)(2,1)S(1)} copy-done((bf16[2,1024,1024]{2,1,0:T(8,128)(2,1)S(1)}, bf16[2,1024,1024]{2,1,0:T(8,128)(2,1)}, u32[]{:S(2)}) %copy-start.1) | copy-done | bytes 4194328
  10.3 0.0 copy-start.5
  10.3 0.0 copy-start.4
  10.3 3.0 %hold.1 = (bf16[2,1024,1024]{2,1,0:T(8,128)(2,1)S(1)}, bf16[2,1024,1024]{2,1,0:T(8,128)(2,1)S(1)}, bf16[2,1024,1024]{2,1,0:T(8,128)(2,1)S(1)}, bf16[2,1024,1024]{2,1,0:T(8,128)(2,1)S(1)}) custom-call(bf16[2,1024,1024]{2,1,0:T(8,128)(2,1)S(1)} %copy-done, bf16[2,1024,1024]{2,1,0:T(8,128)(2,1)S(1)} %copy-done.1), custom_call_target="tpu_custom_call" | custom-call | bytes 25165824 | tf_op jit(solution)/shard_map/hold/pallas_call | solution.py:177
  13.3 0.0 copy-done.5
  13.3 0.0 copy-start.3
  13.3 0.1 broadcast_in_dim.2.scale
  13.4 0.0 collective-permute-done
  13.4 0.2 add_convert_fusion
  13.6 34.3 %all_to_all.27.shares = bf16[8,2,16,1024]{3,2,1,0:T(8,128)(2,1)S(1)} all-to-all(bf16[8,2,16,1024]{3,2,1,0:T(8,128)(2,1)S(1)} %bitcast.13), channel_id=1, replica_groups={{1,129,257,385,513,641,769,897},{65,193,321,449,577,705,833,961},{0,64,..., dimensions={0} | all-to-all | bytes 1048576 | tf_op jit(solution)/shard_map/all_to_all | solution.py:259
  47.8 0.0 copy-done.4
  47.8 1.1 %turn.1 = (f32[2,16,1024]{2,1,0:T(8,128)S(1)}, bf16[512,128]{1,0:T(8,128)(2,1)S(1)}) custom-call(bf16[8,2,16,1024]{3,2,1,0:T(8,128)(2,1)S(1)} %all_to_all.27.shares, f32[2,16,1024]{2,1,0:T(8,128)S(1)} %copy-done.4, bf16[2,1024,1024]{2,1,0:T(8,128)(2,1)S(1)} %get-tuple-element.27.left), custom_call_target="tpu_custom_call" | custom-call | flops 134217728 | bytes 5242880 | tf_op jit(solution)/shard_map/turn/pallas_call | solution.py:190
  48.9 26.0 %all_to_all.28 = bf16[64,8,128]{2,1,0:T(8,128)(2,1)S(1)} all-to-all(bf16[64,8,128]{2,1,0:T(8,128)(2,1)S(1)} %bitcast.12), channel_id=1, replica_groups=mesh['zh'=4,'zl'=2,'xl'=2,'y'=8,'xh'=4,'c'=2] {'y','xh','c'}, dimensions={0} | all-to-all | bytes 262144 | tf_op jit(solution)/shard_map/all_to_all | solution.py:227
  75.0 0.0 copy-done.3
  75.0 1.8 %step.1 = (f32[2,16,1024]{2,1,0:T(8,128)S(1)}, bf16[512,128]{1,0:T(8,128)(2,1)S(1)}) custom-call(bf16[512,128]{1,0:T(8,128)(2,1)S(1)} %bitcast.9, f32[2,16,1024]{2,1,0:T(8,128)S(1)} %copy-done.3, bf16[2,1024,1024]{2,1,0:T(8,128)(2,1)S(1)} %get-tuple-element.29.right, bf16[2,1024,1024]{2,1,0:T(8,128)(2,1)S(1)} %get-tuple-element.30.right_turned), custom_call_target="tpu_custom_call" | custom-call | flops 201326592 | bytes 5242880 | tf_op jit(solution)/shard_map/step/pallas_call | solution.py:202
  76.7 17.1 %all_to_all.29 = bf16[64,8,128]{2,1,0:T(8,128)(2,1)S(1)} all-to-all(bf16[64,8,128]{2,1,0:T(8,128)(2,1)S(1)} %bitcast.11), channel_id=1, replica_groups=mesh['zh'=4,'zl'=2,'xl'=2,'y'=8,'xh'=4,'c'=2] {'y','xh','c'}, dimensions={0} | all-to-all | bytes 262144 | tf_op jit(solution)/shard_map/all_to_all | solution.py:227
  93.8 1.4 %back.1 = (f32[2,16,1024]{2,1,0:T(8,128)}, f32[2,16,1024]{2,1,0:T(8,128)}, f32[2,16,1024]{2,1,0:T(8,128)}) custom-call(f32[2,16,128]{2,1,0:T(8,128)S(1)} %broadcast_in_dim.2.scale, bf16[512,128]{1,0:T(8,128)(2,1)S(1)} %bitcast.10, bf16[2,1024,1024]{2,1,0:T(8,128)(2,1)S(1)} %get-tuple-element.32.left, f32[2,16,1024]{2,1,0:T(8,128)S(1)} %get-tuple-element.33.moment_new, ...), custom_call_target="tpu_custom_call" | custom-call | flops 67108864 | bytes 5242880 | tf_op jit(solution)/shard_map/back/pallas_call | solution.py:214
Async XLA Ops:
  0.6 1.2 %copy-start.2 = (bf16[1,32,16,1024]{3,2,1,0:T(8,128)(2,1)S(1)}, bf16[1,32,16,1024]{3,2,1,0:T(8,128)(2,1)}, u32[]{:S(2)}) copy-start(bf16[1,32,16,1024]{3,2,1,0:T(8,128)(2,1)} %param.6) | copy-start | bytes 3145732
  2.0 11.4 %collective-permute-start = (bf16[4,2,2,16,1024]{4,3,2,1,0:T(8,128)(2,1)S(1)}, bf16[4,2,2,16,1024]{4,3,2,1,0:T(8,128)(2,1)S(1)}, u32[]{:S(2)}, u32[]{:S(2)}) collective-permute-start(bf16[4,2,2,16,1024]{4,3,2,1,0:T(8,128)(2,1)S(1)} %get-tuple-element.26), channel_id=1, source_target_pairs={{0,128},{1,65},{64,192},{65,1},{128,0},{129,193},{192,64},{193,129... | collective-permute-start | bytes 1572872 | tf_op jit(solution)/shard_map/ppermute | solution.py:253
  5.9 2.2 %copy-start = (bf16[2,1024,1024]{2,1,0:T(8,128)(2,1)S(1)}, bf16[2,1024,1024]{2,1,0:T(8,128)(2,1)}, u32[]{:S(2)}) copy-start(bf16[2,1024,1024]{2,1,0:T(8,128)(2,1)} %left.1) | copy-start | bytes 12582916
  8.1 2.2 %copy-start.1 = (bf16[2,1024,1024]{2,1,0:T(8,128)(2,1)S(1)}, bf16[2,1024,1024]{2,1,0:T(8,128)(2,1)}, u32[]{:S(2)}) copy-start(bf16[2,1024,1024]{2,1,0:T(8,128)(2,1)} %right.1) | copy-start | bytes 12582916
  10.3 3.0 %copy-start.5 = (f32[2]{0:T(128)S(1)}, f32[2]{0:T(128)}, u32[]{:S(2)}) copy-start(f32[2]{0:T(128)} %param.11) | copy-start | bytes 28
  10.3 37.5 %copy-start.4 = (f32[2,16,1024]{2,1,0:T(8,128)S(1)}, f32[2,16,1024]{2,1,0:T(8,128)}, u32[]{:S(2)}) copy-start(f32[2,16,1024]{2,1,0:T(8,128)} %moment.1) | copy-start | bytes 393220
  13.3 61.7 %copy-start.3 = (f32[2,16,1024]{2,1,0:T(8,128)S(1)}, f32[2,16,1024]{2,1,0:T(8,128)}, u32[]{:S(2)}) copy-start(f32[2,16,1024]{2,1,0:T(8,128)} %second.1) | copy-start | bytes 393220

commit v9 on v8

--- a/solution.py
+++ b/solution.py
@@ -110,17 +110,24 @@
 
 
 def split_kernel(core, side, parts, away, kept, sems):
-    for index in range(2):
+    mine, other = side[0], 1 - side[0]
+    low, high = pl.ds(0, 2), pl.ds(2, 2)
+    plans = (
+        (
+            (parts.at[low, other], away.at[low]),
+            (parts.at[high, mine], away.at[high]),
+            (parts.at[low, mine], kept.at[low]),
+            (parts.at[high, other], kept.at[high]),
+        ),
+        ((parts.at[:, :, other], away), (parts.at[:, :, mine], kept)),
+    )
+    for index, plan in enumerate(plans):
 
         @pl.when(core[0] == index)
         def _():
-            if index == 1:
-                sources = parts.at[:, :, 1 - side[0]], parts.at[:, :, side[0]]
-            else:
-                sources = parts.at[:, 1 - side[0]], parts.at[:, side[0]]
             copies = [
                 pltpu.make_async_copy(source, out, sems.at[h])
-                for h, (source, out) in enumerate(zip(sources, (away, kept)))
+                for h, (source, out) in enumerate(plan)
             ]
             for copy in copies:
                 copy.start()
@@ -165,7 +172,7 @@
         out_shape=(half, half),
         in_specs=[SMEM, SMEM, ANY],
         out_specs=(ANY, ANY),
-        scratch_shapes=[pltpu.SemaphoreType.DMA((2,))],
+        scratch_shapes=[pltpu.SemaphoreType.DMA((4,))],
         compiler_params=PARAMS,
         cost_estimate=cost(0, 2 << 20),
         name="split",
@@ -235,19 +242,27 @@
     ]
 
 
+def z_set(zh, zl):
+    return (zl + zh // 2) % 2
+
+
 def sum_groups():
     def place(zh, zl, xl, c):
         return 8 * zh + 4 * zl + 2 * xl + c
 
     along_z = [[place(zh, zl, xl, 1) for zh in range(4) for zl in (0, 1)] for xl in (0, 1)]
-    along_x = [[place(zh, zl, xl, 0) for zh in range(4) for xl in (0, 1)] for zl in (0, 1)]
-    return along_z + along_x
+    by_set = [
+        [place(zh, z_set(zh, member), xl, 0) for zh in range(4) for xl in (0, 1)]
+        for member in (0, 1)
+    ]
+    return along_z + by_set
 
 
 def local(grad_parts, momentum, second_moment, left_basis, right_basis, lr_scale):
     parts = grad_parts[0].reshape(4, 2, 2, 2, 16, 1024)
     core = lax.axis_index("c")
-    side = jnp.where(core == 1, lax.axis_index("xl"), lax.axis_index("zl")).reshape(1)
+    member = z_set(lax.axis_index("zh"), lax.axis_index("zl"))
+    side = jnp.where(core == 1, lax.axis_index("xl"), member).reshape(1)
     core = core.reshape(1)
     away, kept = split(core, side, parts)
     came = lax.ppermute(away, NEAR, near_pairs())

time: 95.6 us -> 94.2 us (0.985)
  blocking collectives: 77.4 us -> 75.9 us
    all_to_all x1, blocking collectives: 34.3 us -> 31.2 us  [local(): lax.all_to_all(pair, GROUP, split_axis=0, concat_axis=0, axis_index_group...]
    all_to_all x2, blocking collectives: 43.1 us -> 44.7 us  [trade(): return lax.all_to_all(message, MP, split_axis=0, concat_axis=0, tiled=True)]
where the time goes in v9:
time: 94.2 us; the launch traced here: 93.8 us
  blocking collectives  75.9 us (81%)
  Pallas kernels  7.36 us (8%)
  local copies, waits for them, and re-layouts  5.67 us (6%)
  starting transfers between devices  3.95 us (4%)
    all_to_all x2, blocking collectives, trade(): return lax.all_to_all(message, MP, split_axis=0, concat_axis=0, tiled=True)  44.7 us
    all_to_all x1, blocking collectives, local(): lax.all_to_all(pair, GROUP, split_axis=0, concat_axis=0, axis_index_group...  31.2 us
    unnamed x12, local copies, waits for them, and re-layouts  5.6 us
    ppermute x1, starting transfers between devices, local(): came = lax.ppermute(away, NEAR, near_pairs())  3.95 us
    pallas_call x1, Pallas kernels, hold(): pl.pallas_call(hold_kernel, out_shape=(basis, basis, basis, basis), in_sp...  2.98 us
  transfers between devices with their start and end apart: 1, of which 0 were waited for; matrix products, arithmetic and copies ran while one was open for 0% of the time, Pallas kernels for 3%

profile of v9, /device:TPU:1, one launch (start us, length us, event | category | flops | bytes accessed | tf_op | source)
XLA Modules:
  0.0 93.8 jit_solution(12353966118619393989)
XLA Ops:
  0.7 0.0 copy-start.2
  0.7 1.2 %copy-done.2 = bf16[1,32,16,1024]{3,2,1,0:T(8,128)(2,1)S(1)} copy-done((bf16[1,32,16,1024]{3,2,1,0:T(8,128)(2,1)S(1)}, bf16[1,32,16,1024]{3,2,1,0:T(8,128)(2,1)}, u32[]{:S(2)}) %copy-start.2) | copy-done | bytes 1048600
  1.9 0.1 split.1
  2.0 3.9 %collective-permute-start = (bf16[4,2,2,16,1024]{4,3,2,1,0:T(8,128)(2,1)S(1)}, bf16[4,2,2,16,1024]{4,3,2,1,0:T(8,128)(2,1)S(1)}, u32[]{:S(2)}, u32[]{:S(2)}) collective-permute-start(bf16[4,2,2,16,1024]{4,3,2,1,0:T(8,128)(2,1)S(1)} %get-tuple-element.26), channel_id=1, source_target_pairs={{0,128},{1,65},{64,192},{65,1},{128,0},{129,193},{192,64},{193,129... | collective-permute-start | bytes 1572872 | tf_op jit(solution)/shard_map/ppermute | solution.py:268
  6.0 0.0 copy-start
  6.0 2.2 %copy-done = bf16[2,1024,1024]{2,1,0:T(8,128)(2,1)S(1)} copy-done((bf16[2,1024,1024]{2,1,0:T(8,128)(2,1)S(1)}, bf16[2,1024,1024]{2,1,0:T(8,128)(2,1)}, u32[]{:S(2)}) %copy-start) | copy-done | bytes 4194328
  8.2 0.0 copy-start.1
  8.2 2.2 %copy-done.1 = bf16[2,1024,1024]{2,1,0:T(8,128)(2,1)S(1)} copy-done((bf16[2,1024,1024]{2,1,0:T(8,128)(2,1)S(1)}, bf16[2,1024,1024]{2,1,0:T(8,128)(2,1)}, u32[]{:S(2)}) %copy-start.1) | copy-done | bytes 4194328
  10.3 0.0 copy-start.5
  10.3 0.0 copy-start.4
  10.3 3.0 %hold.1 = (bf16[2,1024,1024]{2,1,0:T(8,128)(2,1)S(1)}, bf16[2,1024,1024]{2,1,0:T(8,128)(2,1)S(1)}, bf16[2,1024,1024]{2,1,0:T(8,128)(2,1)S(1)}, bf16[2,1024,1024]{2,1,0:T(8,128)(2,1)S(1)}) custom-call(bf16[2,1024,1024]{2,1,0:T(8,128)(2,1)S(1)} %copy-done, bf16[2,1024,1024]{2,1,0:T(8,128)(2,1)S(1)} %copy-done.1), custom_call_target="tpu_custom_call" | custom-call | bytes 25165824 | tf_op jit(solution)/shard_map/hold/pallas_call | solution.py:184
  13.3 0.0 copy-done.5
  13.3 0.0 copy-start.3
  13.4 0.1 broadcast_in_dim.2.scale
  13.4 0.0 collective-permute-done
  13.4 0.2 add_convert_fusion
  13.6 31.2 %all_to_all.27.shares = bf16[8,2,16,1024]{3,2,1,0:T(8,128)(2,1)S(1)} all-to-all(bf16[8,2,16,1024]{3,2,1,0:T(8,128)(2,1)S(1)} %bitcast.13), channel_id=1, replica_groups={{1,129,257,385,513,641,769,897},{65,193,321,449,577,705,833,961},{0,64,..., dimensions={0} | all-to-all | bytes 1048576 | tf_op jit(solution)/shard_map/all_to_all | solution.py:274
  44.8 0.0 copy-done.4
  44.8 1.1 %turn.1 = (f32[2,16,1024]{2,1,0:T(8,128)S(1)}, bf16[512,128]{1,0:T(8,128)(2,1)S(1)}) custom-call(bf16[8,2,16,1024]{3,2,1,0:T(8,128)(2,1)S(1)} %all_to_all.27.shares, f32[2,16,1024]{2,1,0:T(8,128)S(1)} %copy-done.4, bf16[2,1024,1024]{2,1,0:T(8,128)(2,1)S(1)} %get-tuple-element.27.left), custom_call_target="tpu_custom_call" | custom-call | flops 134217728 | bytes 5242880 | tf_op jit(solution)/shard_map/turn/pallas_call | solution.py:197
  45.9 27.6 %all_to_all.28 = bf16[64,8,128]{2,1,0:T(8,128)(2,1)S(1)} all-to-all(bf16[64,8,128]{2,1,0:T(8,128)(2,1)S(1)} %bitcast.12), channel_id=1, replica_groups=mesh['zh'=4,'zl'=2,'xl'=2,'y'=8,'xh'=4,'c'=2] {'y','xh','c'}, dimensions={0} | all-to-all | bytes 262144 | tf_op jit(solution)/shard_map/all_to_all | solution.py:234
  73.5 0.0 copy-done.3
  73.5 1.8 %step.1 = (f32[2,16,1024]{2,1,0:T(8,128)S(1)}, bf16[512,128]{1,0:T(8,128)(2,1)S(1)}) custom-call(bf16[512,128]{1,0:T(8,128)(2,1)S(1)} %bitcast.9, f32[2,16,1024]{2,1,0:T(8,128)S(1)} %copy-done.3, bf16[2,1024,1024]{2,1,0:T(8,128)(2,1)S(1)} %get-tuple-element.29.right, bf16[2,1024,1024]{2,1,0:T(8,128)(2,1)S(1)} %get-tuple-element.30.right_turned), custom_call_target="tpu_custom_call" | custom-call | flops 201326592 | bytes 5242880 | tf_op jit(solution)/shard_map/step/pallas_call | solution.py:209
  75.3 17.1 %all_to_all.29 = bf16[64,8,128]{2,1,0:T(8,128)(2,1)S(1)} all-to-all(bf16[64,8,128]{2,1,0:T(8,128)(2,1)S(1)} %bitcast.11), channel_id=1, replica_groups=mesh['zh'=4,'zl'=2,'xl'=2,'y'=8,'xh'=4,'c'=2] {'y','xh','c'}, dimensions={0} | all-to-all | bytes 262144 | tf_op jit(solution)/shard_map/all_to_all | solution.py:234
  92.4 1.4 %back.1 = (f32[2,16,1024]{2,1,0:T(8,128)}, f32[2,16,1024]{2,1,0:T(8,128)}, f32[2,16,1024]{2,1,0:T(8,128)}) custom-call(f32[2,16,128]{2,1,0:T(8,128)S(1)} %broadcast_in_dim.2.scale, bf16[512,128]{1,0:T(8,128)(2,1)S(1)} %bitcast.10, bf16[2,1024,1024]{2,1,0:T(8,128)(2,1)S(1)} %get-tuple-element.32.left, f32[2,16,1024]{2,1,0:T(8,128)S(1)} %get-tuple-element.33.moment_new, ...), custom_call_target="tpu_custom_call" | custom-call | flops 67108864 | bytes 5242880 | tf_op jit(solution)/shard_map/back/pallas_call | solution.py:221
Async XLA Ops:
  0.7 1.2 %copy-start.2 = (bf16[1,32,16,1024]{3,2,1,0:T(8,128)(2,1)S(1)}, bf16[1,32,16,1024]{3,2,1,0:T(8,128)(2,1)}, u32[]{:S(2)}) copy-start(bf16[1,32,16,1024]{3,2,1,0:T(8,128)(2,1)} %param.6) | copy-start | bytes 3145732
  2.0 11.4 %collective-permute-start = (bf16[4,2,2,16,1024]{4,3,2,1,0:T(8,128)(2,1)S(1)}, bf16[4,2,2,16,1024]{4,3,2,1,0:T(8,128)(2,1)S(1)}, u32[]{:S(2)}, u32[]{:S(2)}) collective-permute-start(bf16[4,2,2,16,1024]{4,3,2,1,0:T(8,128)(2,1)S(1)} %get-tuple-element.26), channel_id=1, source_target_pairs={{0,128},{1,65},{64,192},{65,1},{128,0},{129,193},{192,64},{193,129... | collective-permute-start | bytes 1572872 | tf_op jit(solution)/shard_map/ppermute | solution.py:268
  6.0 2.2 %copy-start = (bf16[2,1024,1024]{2,1,0:T(8,128)(2,1)S(1)}, bf16[2,1024,1024]{2,1,0:T(8,128)(2,1)}, u32[]{:S(2)}) copy-start(bf16[2,1024,1024]{2,1,0:T(8,128)(2,1)} %left.1) | copy-start | bytes 12582916
  8.2 2.2 %copy-start.1 = (bf16[2,1024,1024]{2,1,0:T(8,128)(2,1)S(1)}, bf16[2,1024,1024]{2,1,0:T(8,128)(2,1)}, u32[]{:S(2)}) copy-start(bf16[2,1024,1024]{2,1,0:T(8,128)(2,1)} %right.1) | copy-start | bytes 12582916
  10.3 3.0 %copy-start.5 = (f32[2]{0:T(128)S(1)}, f32[2]{0:T(128)}, u32[]{:S(2)}) copy-start(f32[2]{0:T(128)} %param.11) | copy-start | bytes 28
  10.3 34.5 %copy-start.4 = (f32[2,16,1024]{2,1,0:T(8,128)S(1)}, f32[2,16,1024]{2,1,0:T(8,128)}, u32[]{:S(2)}) copy-start(f32[2,16,1024]{2,1,0:T(8,128)} %moment.1) | copy-start | bytes 393220
  13.3 60.1 %copy-start.3 = (f32[2,16,1024]{2,1,0:T(8,128)S(1)}, f32[2,16,1024]{2,1,0:T(8,128)}, u32[]{:S(2)}) copy-start(f32[2,16,1024]{2,1,0:T(8,128)} %second.1) | copy-start | bytes 393220

commit v10 on v8

--- a/solution.py
+++ b/solution.py
@@ -13,7 +13,6 @@
 
 MP = ("y", "xh", "c")
 DP = ("zh", "zl", "xl")
-NEAR = ("zl", "xl", "c")
 GROUP = DP + ("c",)
 F32 = jnp.float32
 BF16 = jnp.bfloat16
@@ -109,23 +108,33 @@
         write.wait()
 
 
+def z_set(z):
+    return (z % 2 + z // 4) % 2
+
+
+def z_members(c, member):
+    return [z for z in range(8) if z_set((z - c) % 8) == member]
+
+
 def split_kernel(core, side, parts, away, kept, sems):
-    for index in range(2):
-
-        @pl.when(core[0] == index)
-        def _():
-            if index == 1:
-                sources = parts.at[:, :, 1 - side[0]], parts.at[:, :, side[0]]
-            else:
-                sources = parts.at[:, 1 - side[0]], parts.at[:, side[0]]
-            copies = [
-                pltpu.make_async_copy(source, out, sems.at[h])
-                for h, (source, out) in enumerate(zip(sources, (away, kept)))
-            ]
-            for copy in copies:
-                copy.start()
-            for copy in copies:
-                copy.wait()
+    def z_of(member, place):
+        first, second = (
+            jnp.where(member == 0, z_members(c, 0)[place], z_members(c, 1)[place]) for c in (0, 1)
+        )
+        return jnp.where(core[0] == 0, first, second)
+
+    copies = []
+    for place in range(4):
+        for member, out in ((1 - side[0], away), (side[0], kept)):
+            copies.append(
+                pltpu.make_async_copy(
+                    parts.at[z_of(member, place)], out.at[place], sems.at[len(copies)]
+                )
+            )
+    for copy in copies:
+        copy.start()
+    for copy in copies:
+        copy.wait()
 
 
 def hold_kernel(left, right, left_held, right_held, right_turned, left_turned, sems):
@@ -165,7 +174,7 @@
         out_shape=(half, half),
         in_specs=[SMEM, SMEM, ANY],
         out_specs=(ANY, ANY),
-        scratch_shapes=[pltpu.SemaphoreType.DMA((2,))],
+        scratch_shapes=[pltpu.SemaphoreType.DMA((8,))],
         compiler_params=PARAMS,
         cost_estimate=cost(0, 2 << 20),
         name="split",
@@ -227,30 +236,35 @@
     return lax.all_to_all(message, MP, split_axis=0, concat_axis=0, tiled=True)
 
 
+def place(z, xl, c):
+    return 4 * z + 2 * xl + c
+
+
 def near_pairs():
-    place = {(zl, xl, c): 4 * zl + 2 * xl + c for zl in (0, 1) for xl in (0, 1) for c in (0, 1)}
     return [
-        (here, place[(zl, 1 - xl, c)] if c == 1 else place[(1 - zl, xl, c)])
-        for (zl, xl, c), here in place.items()
+        (place(z, xl, c), place((((z - c) % 8 ^ 1) + c) % 8, xl, c))
+        for z in range(8)
+        for xl in (0, 1)
+        for c in (0, 1)
     ]
 
 
 def sum_groups():
-    def place(zh, zl, xl, c):
-        return 8 * zh + 4 * zl + 2 * xl + c
-
-    along_z = [[place(zh, zl, xl, 1) for zh in range(4) for zl in (0, 1)] for xl in (0, 1)]
-    along_x = [[place(zh, zl, xl, 0) for zh in range(4) for xl in (0, 1)] for zl in (0, 1)]
-    return along_z + along_x
+    return [
+        [place(z, xl, c) for z in z_members(c, member) for xl in (0, 1)]
+        for c in (0, 1)
+        for member in (0, 1)
+    ]
 
 
 def local(grad_parts, momentum, second_moment, left_basis, right_basis, lr_scale):
-    parts = grad_parts[0].reshape(4, 2, 2, 2, 16, 1024)
+    parts = grad_parts[0].reshape(8, 2, 2, 16, 1024)
     core = lax.axis_index("c")
-    side = jnp.where(core == 1, lax.axis_index("xl"), lax.axis_index("zl")).reshape(1)
+    z = 2 * lax.axis_index("zh") + lax.axis_index("zl")
+    side = z_set((z + 8 - core) % 8).reshape(1)
     core = core.reshape(1)
     away, kept = split(core, side, parts)
-    came = lax.ppermute(away, NEAR, near_pairs())
+    came = lax.ppermute(away, GROUP, near_pairs())
     scale_rows = jnp.broadcast_to(lr_scale[:, None, None], (2, 16, 128))
     held = hold(left_basis, right_basis)
     kept, scale_rows, held = lax.optimization_barrier((kept, scale_rows, held))

time: 95.6 us -> 96.5 us (level)
  blocking collectives: 77.4 us -> 63 us
  starting transfers between devices: 3.95 us -> 17.9 us
  Pallas kernels: 7.34 us -> 8.65 us
    all_to_all x1, blocking collectives: 34.3 us -> 11.3 us  [local(): lax.all_to_all(pair, GROUP, split_axis=0, concat_axis=0, axis_index_group...]
    ppermute x1, starting transfers between devices: 3.95 us -> 17.9 us  [local(): came = lax.ppermute(away, GROUP, near_pairs())]
    all_to_all x2, blocking collectives: 43.1 us -> 51.7 us  [trade(): return lax.all_to_all(message, MP, split_axis=0, concat_axis=0, tiled=True)]
    pallas_call x1, Pallas kernels: 0.09 us -> 1.4 us  [split(): pl.pallas_call(split_kernel, out_shape=(half, half), in_specs=[SMEM, SMEM...]
where the time goes in v10:
time: 96.5 us; the launch traced here: 96.1 us
  blocking collectives  63 us (65%)
  starting transfers between devices  17.9 us (19%)
  Pallas kernels  8.65 us (9%)
  local copies, waits for them, and re-layouts  5.67 us (6%)
    all_to_all x2, blocking collectives, trade(): return lax.all_to_all(message, MP, split_axis=0, concat_axis=0, tiled=True)  51.7 us
    ppermute x1, starting transfers between devices, local(): came = lax.ppermute(away, GROUP, near_pairs())  17.9 us
    all_to_all x1, blocking collectives, local(): lax.all_to_all(pair, GROUP, split_axis=0, concat_axis=0, axis_index_group...  11.3 us
    unnamed x12, local copies, waits for them, and re-layouts  5.6 us
    pallas_call x1, Pallas kernels, hold(): pl.pallas_call(hold_kernel, out_shape=(basis, basis, basis, basis), in_sp...  2.98 us
  transfers between devices with their start and end apart: 1, of which 0 were waited for; matrix products, arithmetic and copies ran while one was open for 0% of the time, Pallas kernels for 3%

profile of v10, /device:TPU:1, one launch (start us, length us, event | category | flops | bytes accessed | tf_op | source)
XLA Modules:
  0.0 96.1 jit_solution(11621512153786930285)
XLA Ops:
  0.7 0.0 copy-start.2
  0.7 1.2 %copy-done.2 = bf16[1,32,16,1024]{3,2,1,0:T(8,128)(2,1)S(1)} copy-done((bf16[1,32,16,1024]{3,2,1,0:T(8,128)(2,1)S(1)}, bf16[1,32,16,1024]{3,2,1,0:T(8,128)(2,1)}, u32[]{:S(2)}) %copy-start.2) | copy-done | bytes 1048600
  1.9 1.4 %split.1 = (bf16[4,2,2,16,1024]{4,3,2,1,0:T(8,128)(2,1)S(1)}, bf16[4,2,2,16,1024]{4,3,2,1,0:T(8,128)(2,1)S(1)}) custom-call(s32[1]{0:T(128)} %bitcast.core, s32[1]{0:T(128)} %bitcast.1.side, bf16[8,2,2,16,1024]{4,3,2,1,0:T(8,128)(2,1)S(1)} %bitcast.8), custom_call_target="tpu_custom_call" | custom-call | bytes 2097152 | tf_op jit(solution)/shard_map/split/pallas_call | solution.py:172
  3.3 17.9 %collective-permute-start = (bf16[4,2,2,16,1024]{4,3,2,1,0:T(8,128)(2,1)S(1)}, bf16[4,2,2,16,1024]{4,3,2,1,0:T(8,128)(2,1)S(1)}, u32[]{:S(2)}, u32[]{:S(2)}) collective-permute-start(bf16[4,2,2,16,1024]{4,3,2,1,0:T(8,128)(2,1)S(1)} %get-tuple-element.26), channel_id=1, source_target_pairs={{0,128},{1,897},{64,192},{65,961},{128,0},{129,257},{192,64},{193,... | collective-permute-start | bytes 1572872 | tf_op jit(solution)/shard_map/ppermute | solution.py:267
  21.2 0.0 copy-start
  21.2 2.2 %copy-done = bf16[2,1024,1024]{2,1,0:T(8,128)(2,1)S(1)} copy-done((bf16[2,1024,1024]{2,1,0:T(8,128)(2,1)S(1)}, bf16[2,1024,1024]{2,1,0:T(8,128)(2,1)}, u32[]{:S(2)}) %copy-start) | copy-done | bytes 4194328
  23.4 0.0 copy-start.1
  23.4 2.2 %copy-done.1 = bf16[2,1024,1024]{2,1,0:T(8,128)(2,1)S(1)} copy-done((bf16[2,1024,1024]{2,1,0:T(8,128)(2,1)S(1)}, bf16[2,1024,1024]{2,1,0:T(8,128)(2,1)}, u32[]{:S(2)}) %copy-start.1) | copy-done | bytes 4194328
  25.6 0.0 copy-start.5
  25.6 0.0 copy-start.4
  25.6 3.0 %hold.1 = (bf16[2,1024,1024]{2,1,0:T(8,128)(2,1)S(1)}, bf16[2,1024,1024]{2,1,0:T(8,128)(2,1)S(1)}, bf16[2,1024,1024]{2,1,0:T(8,128)(2,1)S(1)}, bf16[2,1024,1024]{2,1,0:T(8,128)(2,1)S(1)}) custom-call(bf16[2,1024,1024]{2,1,0:T(8,128)(2,1)S(1)} %copy-done, bf16[2,1024,1024]{2,1,0:T(8,128)(2,1)S(1)} %copy-done.1), custom_call_target="tpu_custom_call" | custom-call | bytes 25165824 | tf_op jit(solution)/shard_map/hold/pallas_call | solution.py:186
  28.6 0.0 copy-done.5
  28.6 0.0 copy-start.3
  28.6 0.1 broadcast_in_dim.2.scale
  28.7 0.0 collective-permute-done
  28.7 0.2 add_convert_fusion
  28.9 11.3 %all_to_all.27.shares = bf16[8,2,16,1024]{3,2,1,0:T(8,128)(2,1)S(1)} all-to-all(bf16[8,2,16,1024]{3,2,1,0:T(8,128)(2,1)S(1)} %bitcast.13), channel_id=1, replica_groups={{0,64,256,320,640,704,896,960},{128,192,384,448,512,576,768,832},{1,65,..., dimensions={0} | all-to-all | bytes 1048576 | tf_op jit(solution)/shard_map/all_to_all | solution.py:273
  40.1 0.0 copy-done.4
  40.1 1.1 %turn.1 = (f32[2,16,1024]{2,1,0:T(8,128)S(1)}, bf16[512,128]{1,0:T(8,128)(2,1)S(1)}) custom-call(bf16[8,2,16,1024]{3,2,1,0:T(8,128)(2,1)S(1)} %all_to_all.27.shares, f32[2,16,1024]{2,1,0:T(8,128)S(1)} %copy-done.4, bf16[2,1024,1024]{2,1,0:T(8,128)(2,1)S(1)} %get-tuple-element.27.left), custom_call_target="tpu_custom_call" | custom-call | flops 134217728 | bytes 5242880 | tf_op jit(solution)/shard_map/turn/pallas_call | solution.py:199
  41.2 34.6 %all_to_all.28 = bf16[64,8,128]{2,1,0:T(8,128)(2,1)S(1)} all-to-all(bf16[64,8,128]{2,1,0:T(8,128)(2,1)S(1)} %bitcast.12), channel_id=1, replica_groups=mesh['zh'=4,'zl'=2,'xl'=2,'y'=8,'xh'=4,'c'=2] {'y','xh','c'}, dimensions={0} | all-to-all | bytes 262144 | tf_op jit(solution)/shard_map/all_to_all | solution.py:236
  75.8 0.0 copy-done.3
  75.8 1.8 %step.1 = (f32[2,16,1024]{2,1,0:T(8,128)S(1)}, bf16[512,128]{1,0:T(8,128)(2,1)S(1)}) custom-call(bf16[512,128]{1,0:T(8,128)(2,1)S(1)} %bitcast.9, f32[2,16,1024]{2,1,0:T(8,128)S(1)} %copy-done.3, bf16[2,1024,1024]{2,1,0:T(8,128)(2,1)S(1)} %get-tuple-element.29.right, bf16[2,1024,1024]{2,1,0:T(8,128)(2,1)S(1)} %get-tuple-element.30.right_turned), custom_call_target="tpu_custom_call" | custom-call | flops 201326592 | bytes 5242880 | tf_op jit(solution)/shard_map/step/pallas_call | solution.py:211
  77.5 17.2 %all_to_all.29 = bf16[64,8,128]{2,1,0:T(8,128)(2,1)S(1)} all-to-all(bf16[64,8,128]{2,1,0:T(8,128)(2,1)S(1)} %bitcast.11), channel_id=1, replica_groups=mesh['zh'=4,'zl'=2,'xl'=2,'y'=8,'xh'=4,'c'=2] {'y','xh','c'}, dimensions={0} | all-to-all | bytes 262144 | tf_op jit(solution)/shard_map/all_to_all | solution.py:236
  94.7 1.4 %back.1 = (f32[2,16,1024]{2,1,0:T(8,128)}, f32[2,16,1024]{2,1,0:T(8,128)}, f32[2,16,1024]{2,1,0:T(8,128)}) custom-call(f32[2,16,128]{2,1,0:T(8,128)S(1)} %broadcast_in_dim.2.scale, bf16[512,128]{1,0:T(8,128)(2,1)S(1)} %bitcast.10, bf16[2,1024,1024]{2,1,0:T(8,128)(2,1)S(1)} %get-tuple-element.32.left, f32[2,16,1024]{2,1,0:T(8,128)S(1)} %get-tuple-element.33.moment_new, ...), custom_call_target="tpu_custom_call" | custom-call | flops 67108864 | bytes 5242880 | tf_op jit(solution)/shard_map/back/pallas_call | solution.py:223
Async XLA Ops:
  0.7 1.2 %copy-start.2 = (bf16[1,32,16,1024]{3,2,1,0:T(8,128)(2,1)S(1)}, bf16[1,32,16,1024]{3,2,1,0:T(8,128)(2,1)}, u32[]{:S(2)}) copy-start(bf16[1,32,16,1024]{3,2,1,0:T(8,128)(2,1)} %param.6) | copy-start | bytes 3145732
  3.3 25.3 %collective-permute-start = (bf16[4,2,2,16,1024]{4,3,2,1,0:T(8,128)(2,1)S(1)}, bf16[4,2,2,16,1024]{4,3,2,1,0:T(8,128)(2,1)S(1)}, u32[]{:S(2)}, u32[]{:S(2)}) collective-permute-start(bf16[4,2,2,16,1024]{4,3,2,1,0:T(8,128)(2,1)S(1)} %get-tuple-element.26), channel_id=1, source_target_pairs={{0,128},{1,897},{64,192},{65,961},{128,0},{129,257},{192,64},{193,... | collective-permute-start | bytes 1572872 | tf_op jit(solution)/shard_map/ppermute | solution.py:267
  21.2 2.2 %copy-start = (bf16[2,1024,1024]{2,1,0:T(8,128)(2,1)S(1)}, bf16[2,1024,1024]{2,1,0:T(8,128)(2,1)}, u32[]{:S(2)}) copy-start(bf16[2,1024,1024]{2,1,0:T(8,128)(2,1)} %left.1) | copy-start | bytes 12582916
  23.4 2.2 %copy-start.1 = (bf16[2,1024,1024]{2,1,0:T(8,128)(2,1)S(1)}, bf16[2,1024,1024]{2,1,0:T(8,128)(2,1)}, u32[]{:S(2)}) copy-start(bf16[2,1024,1024]{2,1,0:T(8,128)(2,1)} %right.1) | copy-start | bytes 12582916
  25.6 3.0 %copy-start.5 = (f32[2]{0:T(128)S(1)}, f32[2]{0:T(128)}, u32[]{:S(2)}) copy-start(f32[2]{0:T(128)} %param.11) | copy-start | bytes 28
  25.6 14.5 %copy-start.4 = (f32[2,16,1024]{2,1,0:T(8,128)S(1)}, f32[2,16,1024]{2,1,0:T(8,128)}, u32[]{:S(2)}) copy-start(f32[2,16,1024]{2,1,0:T(8,128)} %moment.1) | copy-start | bytes 393220
  28.6 47.2 %copy-start.3 = (f32[2,16,1024]{2,1,0:T(8,128)S(1)}, f32[2,16,1024]{2,1,0:T(8,128)}, u32[]{:S(2)}) copy-start(f32[2,16,1024]{2,1,0:T(8,128)} %second.1) | copy-start | bytes 393220
